TPU v7x, 256 devices: a whole 4x4x8 slice. The times are simulated.
256 devices in a mesh: dp: 8 (over z), tensor: 32 (over y, x, core).
Axes of the slice: x: 4, y: 4, z: 8, core: 2. Of those that a mesh axis runs over, the one named last changes fastest.
Arguments:
- activations: bfloat16 [4096, 4096], P('dp', 'tensor'), may hold values from -6 to 6
- cotangent: bfloat16 [4096, 4096], P('dp', 'tensor'), may hold values from -6 to 6
- gate_levels: bfloat16 [4096, 16384], P(None, 'tensor'), may hold values from -1 to 1
- up_levels: bfloat16 [4096, 16384], P(None, 'tensor'), may hold values from -1 to 1
- down_levels: bfloat16 [16384, 4096], P('tensor'), may hold values from -1 to 1
- gate_scales: int32 [64, 16384], P(None, 'tensor'), may hold values from 0 to 255
- up_scales: int32 [64, 16384], P(None, 'tensor'), may hold values from 0 to 255
- down_scales: int32 [256, 4096], P('tensor'), may hold values from 0 to 255
- scale_table: float32 [256], replicated, may hold values from 0.008 to 0.08
- block_pattern: int32 [32, 8, 3], P('tensor'), may hold values from 0 to 127, as said below
- delta_master: float32 [32, 8, 128, 128], P('tensor', 'dp'), may hold values from -0.12 to 0.12
- first_moment: bfloat16 [32, 8, 128, 128], P('tensor', 'dp'), may hold values from -12 to 12
- second_moment: bfloat16 [32, 8, 128, 128], P('tensor', 'dp'), may hold values from 0.049804688 to 5
Outputs:
- layer_output: bfloat16 [4096, 4096], P('dp', 'tensor')
- input_grad: bfloat16 [4096, 4096], P('dp', 'tensor')
- new_delta: float32 [32, 8, 128, 128], P('tensor', 'dp')
- new_first: bfloat16 [32, 8, 128, 128], P('tensor', 'dp')
- new_second: bfloat16 [32, 8, 128, 128], P('tensor', 'dp')
Inputs may be any that keep to these rules, and one draw needn't show every extreme that they name: The blocks of block_pattern[t] are distinct; their hidden block index lies in t * (4) up to (t + 1) * 4 - 1, the width block index below 32, the projection in 0, 1, 2.
All inputs are finite; a program needn't handle non-finite values.
Results may differ from a plain program's by a relative error of at most 0.024.
Values may be sent and summed in bfloat16 or wider, within the bound.
A program may use at most 128 MiB of HBM per device.

v0:
```python
import jax
import jax.numpy as jnp
from jax import lax
from jax.sharding import PartitionSpec as P

BLK = 128
QBLK = 64
ADAM_STEP = 20


beta_one = 0.9
beta_two = 0.999
adam_eps = 1e-08
learn_rate = 0.05


def lookup_scales(scale_codes, scale_table):

    def lookup_visit(level_index, running):
        return jnp.where(scale_codes == level_index, scale_table[level_index], running)

    return lax.fori_loop(
        0, scale_table.shape[0], lookup_visit, jnp.zeros(scale_codes.shape, jnp.float32)
    )


def dequantize(levels, scale_codes, scale_table):
    row_total, col_total = levels.shape
    scales = lookup_scales(scale_codes, scale_table)
    grouped = (
        levels.astype(jnp.float32).reshape(row_total // QBLK, QBLK, col_total) * scales[:, None, :]
    )
    return grouped.reshape(row_total, col_total).astype(jnp.bfloat16)


def add_blocks(weights, pattern, blocks, ff_offset):

    def add_visit(slot_index, carried):
        gate_w, up_w, down_w = carried
        matrix = pattern[slot_index, 0]
        width_at = pattern[slot_index, 1] * BLK
        hidden_at = pattern[slot_index, 2] * BLK - ff_offset
        delta_block = blocks[slot_index].astype(jnp.float32)

        def apply(weight, target, row_at, col_at):
            current = lax.dynamic_slice(weight, (row_at, col_at), (BLK, BLK))
            updated = jnp.where(
                matrix == target,
                (current.astype(jnp.float32) + delta_block).astype(jnp.bfloat16),
                current,
            )
            return lax.dynamic_update_slice(weight, updated, (row_at, col_at))

        return (
            apply(gate_w, 0, width_at, hidden_at),
            apply(up_w, 1, width_at, hidden_at),
            apply(down_w, 2, hidden_at, width_at),
        )

    return lax.fori_loop(0, pattern.shape[0], add_visit, weights)


def local(
    activations,
    cotangent,
    gate_levels,
    up_levels,
    down_levels,
    gate_scales,
    up_scales,
    down_scales,
    scale_table,
    block_pattern,
    delta_master,
    first_moment,
    second_moment,
):
    used_blocks = lax.all_gather(delta_master.astype(jnp.bfloat16), "dp", axis=1, tiled=True)
    pattern = block_pattern[0]
    blocks = used_blocks[0]
    ff_width = gate_levels.shape[1]
    ff_offset = lax.axis_index("tensor") * ff_width
    weights = (
        dequantize(gate_levels, gate_scales, scale_table),
        dequantize(up_levels, up_scales, scale_table),
        dequantize(down_levels, down_scales, scale_table),
    )
    gate_w, up_w, down_w = add_blocks(weights, pattern, blocks, ff_offset)
    whole_x = lax.all_gather(activations, "tensor", axis=1, tiled=True)
    gate_pre = jnp.dot(whole_x, gate_w, preferred_element_type=jnp.float32)
    up_pre = jnp.dot(whole_x, up_w, preferred_element_type=jnp.float32)
    sigmoid_gate = jax.nn.sigmoid(gate_pre)
    hidden = (gate_pre * sigmoid_gate * up_pre).astype(jnp.bfloat16)
    contract_last = (((1,), (1,)), ((), ()))
    contract_first = (((0,), (0,)), ((), ()))
    whole_dy = lax.all_gather(cotangent, "tensor", axis=1, tiled=True)
    grad_hidden = lax.dot_general(
        whole_dy, down_w, contract_last, preferred_element_type=jnp.float32
    )
    grad_up = (grad_hidden * gate_pre * sigmoid_gate).astype(jnp.bfloat16)
    grad_gate = (
        grad_hidden * up_pre * sigmoid_gate * (1.0 + gate_pre * (1.0 - sigmoid_gate))
    ).astype(jnp.bfloat16)
    output_part = lax.psum_scatter(
        lax.dot_general(
            down_w, hidden, (((0,), (1,)), ((), ())), preferred_element_type=jnp.float32
        ).astype(jnp.bfloat16),
        "tensor",
        scatter_dimension=0,
        tiled=True,
    ).astype(jnp.float32)
    from_gate = lax.dot_general(
        gate_w, grad_gate, contract_last, preferred_element_type=jnp.float32
    )
    from_up = lax.dot_general(up_w, grad_up, contract_last, preferred_element_type=jnp.float32)
    input_part = lax.psum_scatter(
        (from_gate + from_up).astype(jnp.bfloat16), "tensor", scatter_dimension=0, tiled=True
    ).astype(jnp.float32)
    layer_output = output_part.T.astype(jnp.bfloat16)
    input_grad = input_part.T.astype(jnp.bfloat16)

    def slot_grad(slot_index, collected):
        matrix = pattern[slot_index, 0]
        width_at = pattern[slot_index, 1] * BLK
        hidden_at = pattern[slot_index, 2] * BLK - ff_offset
        x_part = lax.dynamic_slice_in_dim(whole_x, width_at, BLK, 1)
        dy_part = lax.dynamic_slice_in_dim(whole_dy, width_at, BLK, 1)
        gate_part = lax.dynamic_slice_in_dim(grad_gate, hidden_at, BLK, 1)
        up_part = lax.dynamic_slice_in_dim(grad_up, hidden_at, BLK, 1)
        hidden_part = lax.dynamic_slice_in_dim(hidden, hidden_at, BLK, 1)
        for_gate = lax.dot_general(
            x_part, gate_part, contract_first, preferred_element_type=jnp.float32
        )
        for_up = lax.dot_general(
            x_part, up_part, contract_first, preferred_element_type=jnp.float32
        )
        for_down = lax.dot_general(
            hidden_part, dy_part, contract_first, preferred_element_type=jnp.float32
        )
        chosen = jnp.where(matrix == 0, for_gate, jnp.where(matrix == 1, for_up, for_down))
        return lax.dynamic_update_slice(collected, chosen[None], (slot_index, 0, 0))

    slot_total = pattern.shape[0]
    block_grads = lax.fori_loop(
        0, slot_total, slot_grad, jnp.zeros((slot_total, BLK, BLK), jnp.float32)
    )[None]
    owned = delta_master.shape[1]
    total_grads = lax.psum(block_grads.astype(jnp.bfloat16), "dp").astype(jnp.float32)
    own_grads = lax.dynamic_slice_in_dim(total_grads, lax.axis_index("dp") * owned, owned, 1)
    moment = beta_one * first_moment.astype(jnp.float32) + (1.0 - beta_one) * own_grads
    second = beta_two * second_moment.astype(jnp.float32) + (1.0 - beta_two) * own_grads * own_grads
    bias_one = 1.0 - beta_one**ADAM_STEP
    bias_two = 1.0 - beta_two**ADAM_STEP
    step_size = learn_rate * (moment / bias_one) / (jnp.sqrt(second / bias_two) + adam_eps)
    new_delta = delta_master - step_size
    return (
        layer_output,
        input_grad,
        new_delta,
        moment.astype(jnp.bfloat16),
        second.astype(jnp.bfloat16),
    )


def solution(mesh):
    in_specs = (
        P("dp", "tensor"),
        P("dp", "tensor"),
        P(None, "tensor"),
        P(None, "tensor"),
        P("tensor", None),
        P(None, "tensor"),
        P(None, "tensor"),
        P("tensor", None),
        P(),
        P("tensor", None, None),
        P("tensor", "dp", None, None),
        P("tensor", "dp", None, None),
        P("tensor", "dp", None, None),
    )
    out_specs = (
        P("dp", "tensor"),
        P("dp", "tensor"),
        P("tensor", "dp", None, None),
        P("tensor", "dp", None, None),
        P("tensor", "dp", None, None),
    )
    return jax.shard_map(local, mesh=mesh, in_specs=in_specs, out_specs=out_specs, check_vma=False)
```

profile of v0, /device:TPU:32, one launch (start us, length us, event | category | flops | bytes accessed | tf_op | source)
XLA Modules:
  0.0 2410.8 jit_solution(3403175529737707075)
XLA Ops:
  8.7 736.3 %while.74 = (s32[]{:T(128)}, f32[64,512]{1,0:T(8,128)S(1)}, s32[64,512]{1,0:T(8,128)}, f32[256]{0:T(256)}, s32[]{:T(128)}, /*index=5*/s32[]{:T(128)}) while((s32[]{:T(128)}, f32[64,512]{1,0:T(8,128)S(1)}, s32[64,512]{1,0:T(8,128)}, f32[256]{0:T(256)}, s32[]{:T(128)}, /*index=5*/s32[]{:T(128)}) %tuple.160), condition=%wide.region_1.2_spmd.clone, body=%wide.region_0.1_spmd.clone.sunk | while | flops 98307 | bytes 393315 | solution.py:22
  47.4 1.7 select_select_fusion.6
  59.0 1.6 select_select_fusion.6
  105.0 1.6 select_select_fusion.6
  110.8 1.7 select_select_fusion.6
  119.5 1.6 select_select_fusion.6
  745.0 734.7 %while.76 = (s32[]{:T(128)}, f32[8,4096]{1,0:T(8,128)S(1)}, s32[8,4096]{1,0:T(8,128)}, f32[256]{0:T(256)}, s32[]{:T(128)}, /*index=5*/s32[]{:T(128)}) while((s32[]{:T(128)}, f32[8,4096]{1,0:T(8,128)S(1)}, s32[8,4096]{1,0:T(8,128)}, f32[256]{0:T(256)}, s32[]{:T(128)}, /*index=5*/s32[]{:T(128)}) %tuple.186), condition=%wide.region_5.6_spmd.clone, body=%wide.region_4.5_spmd.clone.sunk | while | flops 98307 | bytes 393315 | solution.py:22
  1479.8 505.5 %while.75 = (s32[]{:T(128)}, f32[64,512]{1,0:T(8,128)S(1)}, s32[64,512]{1,0:T(8,128)S(1)}, f32[256]{0:T(256)}, s32[]{:T(128)}, /*index=5*/s32[]{:T(128)}) while((s32[]{:T(128)}, f32[64,512]{1,0:T(8,128)S(1)}, s32[64,512]{1,0:T(8,128)S(1)}, f32[256]{0:T(256)}, s32[]{:T(128)}, /*index=5*/s32[]{:T(128)}) %tuple.187), condition=%wide.region_3.4_spmd.clone, body=%wide.region_2.3_spmd.clone.sunk | while | flops 98307 | bytes 393315 | solution.py:22
  1985.4 5.5 fusion.21
  1990.9 4.4 fusion.22
  1995.3 27.6 %all_gather.9 = bf16[1,8,128,128]{3,2,0,1:T(8,128)(2,1)S(1)} all-gather(bf16[1,1,128,128]{3,2,0,1:T(8,128)(2,1)S(1)} %bitcast_convert_fusion), channel_id=1, replica_groups=mesh['dp'=8,'tensor'=32] {'dp'}, dimensions={1}, use_global_device_ids=true | all-gather | bytes 294912 | tf_op jit(solution)/shard_map/all_gather | solution.py:78
  2022.9 42.9 %while.72 = (s32[]{:T(128)}, bf16[4096,512]{1,0:T(8,128)(2,1)}, bf16[4096,512]{1,0:T(8,128)(2,1)}, bf16[512,4096]{1,0:T(8,128)(2,1)}, s32[8,3]{0,1:T(4,128)S(1)}...) while((s32[]{:T(128)}, bf16[4096,512]{1,0:T(8,128)(2,1)}, ...), condition=%wide.region_7.8_spmd, body=%wide.region_6.7_spmd.sunk | while | flops 213006 | bytes 231732 | solution.py:60
  2065.8 6.0 convolution_bitcast_fusion.1
  2071.8 3.4 convolution_bitcast_fusion.2
  2075.2 6.6 multiply_convert_fusion
  2081.8 5.6 fusion.28
  2087.4 57.5 %while.73 = (s32[]{:T(128)}, bf16[8,128,128]{2,1,0:T(8,128)(2,1)}, s32[8,3]{0,1:T(4,128)S(1)}, bf16[512,4096]{1,0:T(8,128)(2,1)}, s32[]{:T(128)}, /*index=5*/bf1...) while((s32[]{:T(128)}, bf16[8,128,128]{2,1,0:T(8,128)(2,1)}, ...), condition=%wide.region_11.12_spmd, body=%wide.region_10.11_spmd.sunk | while | flops 50364428 | bytes 952131 | solution.py:144
  2092.9 1.7 fusion.58
  2100.1 1.7 fusion.58
  2107.2 1.7 fusion.58
  2114.4 1.7 fusion.58
  2121.6 1.7 fusion.58
  2128.8 1.8 fusion.58
  2136.0 1.7 fusion.58
  2143.2 1.7 fusion.58
  2145.0 9.0 add_convert_fusion
  2154.3 6.6 convolution_convert_fusion
  2160.8 56.4 %all-reduce.2.cloned.1.call-done = bf16[1,8,128,128]{3,2,1,0:T(8,128)(2,1)} async-done(((bf16[1,8,128,128]{3,2,1,0:T(8,128)(2,1)}), bf16[1,8,128,128]{3,2,1,0:T(8,128)(2,1)}) %all-reduce.2.cloned.1.call-update) | async-done | bytes 262160 | tf_op jit(solution)/shard_map/psum | solution.py:148
  2218.8 91.0 %reduce-scatter.5.cloned.1.call-done = bf16[128,512]{1,0:T(8,128)(2,1)} async-done(((bf16[4096,512]{1,0:T(8,128)(2,1)}), bf16[128,512]{1,0:T(8,128)(2,1)}) %reduce-scatter.5.cloned.1.call-update) | async-done | bytes 131088 | tf_op jit(solution)/shard_map/reduce_scatter | solution.py:116
  2309.8 1.7 copy.28
  2311.4 91.1 %reduce-scatter.3.cloned.1.call-done = bf16[128,512]{1,0:T(8,128)(2,1)} async-done(((bf16[4096,512]{1,0:T(8,128)(2,1)}), bf16[128,512]{1,0:T(8,128)(2,1)}) %reduce-scatter.3.cloned.1.call-update) | async-done | bytes 131088 | tf_op jit(solution)/shard_map/reduce_scatter | solution.py:104
  2402.6 1.7 copy.27
  (1610 shorter events, 1995.9 us)
Async XLA Ops:
  7.2 1472.6 %copy-start.4 = (s32[64,512]{1,0:T(8,128)S(1)}, s32[64,512]{1,0:T(8,128)}, u32[]{:S(2)}) copy-start(s32[64,512]{1,0:T(8,128)} %param.29) | copy-start | bytes 393220
  7.2 1978.2 %copy-start.9 = (s32[1,8,3]{1,0,2:T(1,128)S(1)}, s32[1,8,3]{1,0,2:T(1,128)}, u32[]{:S(2)}) copy-start(s32[1,8,3]{1,0,2:T(1,128)} %param.32) | copy-start | bytes 292
  7.2 2058.6 %all-gather.3.cloned.1.call-start = ((), (), s32[]{:S(2)}) async-start(), calls=%async_computation.2 | async-start | bytes 4325376 | tf_op jit(solution)/shard_map/all_gather | solution.py:89
  7.9 2067.3 %all-gather.5.cloned.1.call-start = ((), (), s32[]{:S(2)}) async-start(), calls=%async_computation.4 | async-start | bytes 4325376 | tf_op jit(solution)/shard_map/all_gather | solution.py:96
  8.7 2208.6 %all-reduce.2.cloned.1.call-start = ((), (), s32[]{:S(2)}) async-start(), calls=%async_computation.6 | async-start | bytes 524288 | tf_op jit(solution)/shard_map/psum | solution.py:148
  1985.4 5.5 copy-start.2
  1985.4 5.5 copy-start.3
  1990.9 4.4 copy-start.6
  2065.8 6.0 copy-start
  2065.8 6.0 copy-start.5
  2075.2 6.6 copy-start.1
  2144.9 164.8 %reduce-scatter.5.cloned.1.call-start = ((), (), s32[]{:S(2)}) async-start(), calls=%async_computation.5 | async-start | bytes 4325376 | tf_op jit(solution)/shard_map/reduce_scatter | solution.py:116
  2154.0 248.6 %reduce-scatter.3.cloned.1.call-start = ((), (), s32[]{:S(2)}) async-start(), calls=%async_computation.3 | async-start | bytes 4325376 | tf_op jit(solution)/shard_map/reduce_scatter | solution.py:104
  2160.8 56.5 %copy-start.7 = (bf16[1,1,128,128]{3,2,1,0:T(8,128)(2,1)S(1)}, bf16[1,1,128,128]{3,2,1,0:T(8,128)(2,1)}, u32[]{:S(2)}) copy-start(bf16[1,1,128,128]{3,2,1,0:T(8,128)(2,1)} %param.35) | copy-start | bytes 98308
  2160.8 56.5 %copy-start.8 = (bf16[1,1,128,128]{3,2,1,0:T(8,128)(2,1)S(1)}, bf16[1,1,128,128]{3,2,1,0:T(8,128)(2,1)}, u32[]{:S(2)}) copy-start(bf16[1,1,128,128]{3,2,1,0:T(8,128)(2,1)} %param.34) | copy-start | bytes 98308
Sparse Core Ops, SparseCore 0:
  10.5 56.8 all-gather.2
  69.9 54.0 all-gather.4
  2145.1 72.1 all-reduce.1
  2221.6 88.1 reduce-scatter.4
  2313.5 88.9 reduce-scatter.2
where the time goes:
time: 2440 us; the launch traced here: 2410 us
  other arithmetic  1010 us (41%)
  local copies, waits for them, and re-layouts  985 us (40%)
  waiting for transfers between devices  240 us (10%)
  matrix products  68.8 us (3%)
  loops' own time  62.3 us (3%)
  blocking collectives  27.6 us (1%)
    select_n x768, other arithmetic, lookup_visit(): jnp.where(scale_codes == level_index, scale_table[level_index], running)  989 us
    dynamic_slice x768, local copies, waits for them, and re-layouts, lookup_visit(): scale_table[level_index]  972 us
    reduce_scatter x1, waiting for transfers between devices, local(): lax.psum_scatter(lax.dot_general(down_w, hidden, (((0,), (1,)), ((), ()))...  91.1 us
    reduce_scatter x1, waiting for transfers between devices, local(): lax.psum_scatter((from_gate + from_up).astype(jnp.bfloat16), 'tensor', sc...  91 us
    psum x1, waiting for transfers between devices, local(): lax.psum(block_grads.astype(jnp.bfloat16), 'dp').astype(jnp.float32)  56.4 us
  transfers between devices with their start and end apart: 5, of which 3 were waited for; matrix products, arithmetic and copies ran while one was open for 84% of the time, Pallas kernels for 0%

commit v1 on v0

--- a/solution.py
+++ b/solution.py
@@ -1,6 +1,8 @@
 import jax
 import jax.numpy as jnp
 from jax import lax
+from jax.experimental import pallas as pl
+from jax.experimental.pallas import tpu as pltpu
 from jax.sharding import PartitionSpec as P
 
 BLK = 128
@@ -14,50 +16,94 @@
 learn_rate = 0.05
 
 
-def lookup_scales(scale_codes, scale_table):
-
-    def lookup_visit(level_index, running):
-        return jnp.where(scale_codes == level_index, scale_table[level_index], running)
-
-    return lax.fori_loop(
-        0, scale_table.shape[0], lookup_visit, jnp.zeros(scale_codes.shape, jnp.float32)
-    )
-
-
-def dequantize(levels, scale_codes, scale_table):
-    row_total, col_total = levels.shape
-    scales = lookup_scales(scale_codes, scale_table)
-    grouped = (
-        levels.astype(jnp.float32).reshape(row_total // QBLK, QBLK, col_total) * scales[:, None, :]
-    )
-    return grouped.reshape(row_total, col_total).astype(jnp.bfloat16)
-
-
-def add_blocks(weights, pattern, blocks, ff_offset):
-
-    def add_visit(slot_index, carried):
-        gate_w, up_w, down_w = carried
-        matrix = pattern[slot_index, 0]
-        width_at = pattern[slot_index, 1] * BLK
-        hidden_at = pattern[slot_index, 2] * BLK - ff_offset
-        delta_block = blocks[slot_index].astype(jnp.float32)
-
-        def apply(weight, target, row_at, col_at):
-            current = lax.dynamic_slice(weight, (row_at, col_at), (BLK, BLK))
-            updated = jnp.where(
-                matrix == target,
-                (current.astype(jnp.float32) + delta_block).astype(jnp.bfloat16),
-                current,
+def take_scales(codes, table_ref):
+    low = jnp.broadcast_to(table_ref[0:1, :], codes.shape)
+    high = jnp.broadcast_to(table_ref[1:2, :], codes.shape)
+    within = jnp.bitwise_and(codes, 127)
+    from_low = jnp.take_along_axis(low, within, axis=1, mode="promise_in_bounds")
+    from_high = jnp.take_along_axis(high, within, axis=1, mode="promise_in_bounds")
+    return jnp.where(codes < 128, from_low, from_high)
+
+
+def scale_tile(levels, upper, lower, block):
+    scales = jnp.concatenate(
+        [jnp.broadcast_to(upper, (QBLK, BLK)), jnp.broadcast_to(lower, (QBLK, BLK))], axis=0
+    )
+    base = (levels.astype(jnp.float32) * scales).astype(jnp.bfloat16)
+    return (base.astype(jnp.float32) + block.astype(jnp.float32)).astype(jnp.bfloat16)
+
+
+def weights_kernel(
+    gate_ref, up_ref, down_ref, gate_codes, up_codes, down_codes, table_ref, slot_of, blocks_ref,
+    gate_out, up_out, down_out,
+):
+    width_count = gate_ref.shape[0] // BLK
+    hidden_count = gate_ref.shape[1] // BLK
+
+    for which, levels_ref, codes_ref, out_ref in (
+        (0, gate_ref, gate_codes, gate_out), (1, up_ref, up_codes, up_out)
+    ):
+        @pl.loop(0, width_count // 4)
+        def _(group):
+            for hidden_at in range(hidden_count):
+                lanes = pl.ds(hidden_at * BLK, BLK)
+                codes = codes_ref[pl.ds(pl.multiple_of(group * 8, 8), 8), lanes]
+                scales = take_scales(codes, table_ref)
+                for inner in range(4):
+                    at = group * 4 + inner
+                    rows = pl.ds(pl.multiple_of(at * BLK, BLK), BLK)
+                    slot = slot_of[(which * width_count + at) * hidden_count + hidden_at]
+                    out_ref[rows, lanes] = scale_tile(
+                        levels_ref[rows, lanes], scales[2 * inner : 2 * inner + 1],
+                        scales[2 * inner + 1 : 2 * inner + 2], blocks_ref[slot],
+                    )
+
+    @pl.loop(0, width_count)
+    def _(at):
+        lanes = pl.ds(pl.multiple_of(at * BLK, BLK), BLK)
+        scales = take_scales(down_codes[:, lanes], table_ref)
+        for hidden_at in range(hidden_count):
+            rows = pl.ds(hidden_at * BLK, BLK)
+            slot = slot_of[(2 * width_count + at) * hidden_count + hidden_at]
+            down_out[rows, lanes] = scale_tile(
+                down_ref[rows, lanes], scales[2 * hidden_at : 2 * hidden_at + 1],
+                scales[2 * hidden_at + 1 : 2 * hidden_at + 2], blocks_ref[slot],
             )
-            return lax.dynamic_update_slice(weight, updated, (row_at, col_at))
-
-        return (
-            apply(gate_w, 0, width_at, hidden_at),
-            apply(up_w, 1, width_at, hidden_at),
-            apply(down_w, 2, hidden_at, width_at),
-        )
-
-    return lax.fori_loop(0, pattern.shape[0], add_visit, weights)
+
+
+def slot_map(pattern, width_count, hidden_count, hidden_first):
+    slots = pattern.shape[0]
+    place = (pattern[:, 0] * width_count + pattern[:, 1]) * hidden_count + (
+        pattern[:, 2] - hidden_first
+    )
+    tiles = jnp.arange(3 * width_count * hidden_count, dtype=jnp.int32)
+    found = jnp.where(
+        place[:, None] == tiles[None, :], jnp.arange(slots, dtype=jnp.int32)[:, None], slots
+    )
+    return jnp.min(found, axis=0)
+
+
+def used_weights(
+    gate_levels, up_levels, down_levels, gate_scales, up_scales, down_scales, scale_table,
+    pattern, blocks,
+):
+    hidden_count = gate_levels.shape[1] // BLK
+    slot_of = slot_map(
+        pattern, gate_levels.shape[0] // BLK, hidden_count, lax.axis_index("tensor") * hidden_count
+    )
+    padded = jnp.concatenate([blocks, jnp.zeros((1, BLK, BLK), blocks.dtype)], axis=0)
+    whole = pl.BlockSpec(memory_space=pltpu.VMEM)
+    return pl.pallas_call(
+        weights_kernel,
+        out_shape=[jax.ShapeDtypeStruct(v.shape, v.dtype) for v in (gate_levels, up_levels, down_levels)],
+        in_specs=[whole] * 7 + [pl.BlockSpec(memory_space=pltpu.SMEM), whole],
+        out_specs=[whole] * 3,
+        compiler_params=pltpu.CompilerParams(vmem_limit_bytes=48 * 1024 * 1024),
+        cost_estimate=pl.CostEstimate(flops=12_000_000, bytes_accessed=30_000_000, transcendentals=0),
+    )(
+        gate_levels, up_levels, down_levels, gate_scales, up_scales, down_scales,
+        scale_table.reshape(2, 128), slot_of, padded,
+    )
 
 
 def local(
@@ -80,12 +126,10 @@
     blocks = used_blocks[0]
     ff_width = gate_levels.shape[1]
     ff_offset = lax.axis_index("tensor") * ff_width
-    weights = (
-        dequantize(gate_levels, gate_scales, scale_table),
-        dequantize(up_levels, up_scales, scale_table),
-        dequantize(down_levels, down_scales, scale_table),
-    )
-    gate_w, up_w, down_w = add_blocks(weights, pattern, blocks, ff_offset)
+    gate_w, up_w, down_w = used_weights(
+        gate_levels, up_levels, down_levels, gate_scales, up_scales, down_scales, scale_table,
+        pattern, blocks,
+    )
     whole_x = lax.all_gather(activations, "tensor", axis=1, tiled=True)
     gate_pre = jnp.dot(whole_x, gate_w, preferred_element_type=jnp.float32)
     up_pre = jnp.dot(whole_x, up_w, preferred_element_type=jnp.float32)

time: 2440 us -> 460 us (0.19); the launches traced: 2410 us -> 459 us
  other arithmetic: 1010 us -> 2.4 us
  local copies, waits for them, and re-layouts: 985 us -> 14.1 us
  waiting for transfers between devices: 240 us -> 294 us
  loops' own time: 62.3 us -> 21.1 us
    select_n x768 -> x0, other arithmetic: 989 us -> none  [lookup_visit(): jnp.where(scale_codes == level_index, scale_table[level_index], running)]
    dynamic_slice x776 -> x0, local copies, waits for them, and re-layouts: 977 us -> none  [the longest x768 972 us: lookup_visit(): scale_table[level_index]]
    all_gather x1, waiting for transfers between devices: 0.01 us -> 47 us  [local(): whole_dy = lax.all_gather(cotangent, 'tensor', axis=1, tiled=True)]
    another operation x4 -> x0, loops' own time: 41.3 us -> none  [the longest x1 25.9 us: add_blocks(): return lax.fori_loop(0, pattern.shape[0], add_visit, weights)]
  transfers between devices with their start and end apart: 5 -> 5, of which waited for: 3 -> 5; matrix products, arithmetic and copies ran while one was open for 84% -> 6% of each run, Pallas kernels for 0% -> 4%
where the time goes in v1:
time: 460 us; the launch traced here: 459 us
  waiting for transfers between devices  294 us (64%)
  matrix products  68.6 us (15%)
  blocking collectives  27.5 us (6%)
  loops' own time  21.1 us (5%)
  Pallas kernels  17.4 us (4%)
  local copies, waits for them, and re-layouts  14.1 us (3%)
  between operations  13.9 us (3%)
    reduce_scatter x1, waiting for transfers between devices, local(): lax.psum_scatter(lax.dot_general(down_w, hidden, (((0,), (1,)), ((), ()))...  91.1 us
    reduce_scatter x1, waiting for transfers between devices, local(): lax.psum_scatter((from_gate + from_up).astype(jnp.bfloat16), 'tensor', sc...  91 us
    psum x1, waiting for transfers between devices, local(): lax.psum(block_grads.astype(jnp.bfloat16), 'dp').astype(jnp.float32)  56.3 us
    all_gather x1, waiting for transfers between devices, local(): whole_dy = lax.all_gather(cotangent, 'tensor', axis=1, tiled=True)  47 us
    all_gather x1, blocking collectives, local(): lax.all_gather(delta_master.astype(jnp.bfloat16), 'dp', axis=1, tiled=True)  27.5 us
    another operation x1, loops' own time, local(): lax.fori_loop(0, slot_total, slot_grad, jnp.zeros((slot_total, BLK, BLK),...  21.1 us
    pallas_call x1, Pallas kernels, used_weights(): pl.pallas_call(weights_kernel, out_shape=[jax.ShapeDtypeStruct(v.shape, v...  17.4 us
    dot_general x8, matrix products, slot_grad(): lax.dot_general(x_part, gate_part, contract_first, preferred_element_type...  14 us
  transfers between devices with their start and end apart: 5, of which 5 were waited for; matrix products, arithmetic and copies ran while one was open for 6% of the time, Pallas kernels for 4%

profile of v1, /device:TPU:32, one launch (start us, length us, event | category | flops | bytes accessed | tf_op | source)
XLA Modules:
  0.0 459.0 jit_solution(11137823456910965699)
XLA Ops:
  10.2 27.5 %all_gather.9 = bf16[1,8,128,128]{3,2,0,1:T(8,128)(2,1)S(1)} all-gather(bf16[1,1,128,128]{3,2,0,1:T(8,128)(2,1)S(1)} %bitcast_convert_fusion), channel_id=1, replica_groups=mesh['dp'=8,'tensor'=32] {'dp'}, dimensions={1}, use_global_device_ids=true | all-gather | bytes 294912 | tf_op jit(solution)/shard_map/all_gather | solution.py:124
  41.3 17.4 %shard_map.164 = (bf16[4096,512]{1,0:T(8,128)(2,1)S(1)}, bf16[4096,512]{1,0:T(8,128)(2,1)}, bf16[512,4096]{1,0:T(8,128)(2,1)}) custom-call(bf16[4096,512]{1,0:T(8,128)(2,1)} %gate_ref.1, bf16[4096,512]{1,0:T(8,128)(2,1)} %up_ref.1, bf16[512,4096]{1,0:T(8,128)(2,1)} %down_ref.1, s32[64,512]{1,0:T(8,128)S(1)} %copy-done.3, s32[64,512]{1,0:T(8,128)S(1)} %copy-done.4, ...), custom_call_target="tpu_custom_call" | custom-call | flops 12000000 | bytes 30000000 | tf_op jit(solution)/shard_map/pallas_call | solution.py:96
  58.7 2.0 copy-done
  60.6 6.7 %all-gather.3.cloned.1.call-done = bf16[512,4096]{1,0:T(8,128)(2,1)} async-done(((bf16[512,128]{1,0:T(8,128)(2,1)}), bf16[512,4096]{1,0:T(8,128)(2,1)}) %all-gather.3.cloned.1.call-update) | async-done | bytes 4194320 | tf_op jit(solution)/shard_map/all_gather | solution.py:133
  67.4 6.0 %convolution_bitcast_fusion.1 = f32[512,512]{0,1:T(8,128)S(1)} fusion(bf16[4096,512]{1,0:T(8,128)(2,1)} %get-tuple-element.164, bf16[512,4096]{1,0:T(8,128)(2,1)} %all-gather.3.cloned.1.call-done), kind=kOutput, calls=%fused_computation.20 | convolution fusion | flops 2147483648 | bytes 9437184 | tf_op jit(solution)/shard_map/dot_general | solution.py:135
  73.3 3.3 convolution_bitcast_fusion.2
  76.7 47.0 %all-gather.5.cloned.1.call-done = bf16[512,4096]{1,0:T(8,128)(2,1)} async-done(((bf16[512,128]{1,0:T(8,128)(2,1)}), bf16[512,4096]{1,0:T(8,128)(2,1)}) %all-gather.5.cloned.1.call-update) | async-done | bytes 4194320 | tf_op jit(solution)/shard_map/all_gather | solution.py:140
  123.7 6.6 %multiply_convert_fusion = (bf16[512,512]{0,1:T(8,128)(2,1)S(1)}, bf16[512,512]{0,1:T(8,128)(2,1)S(1)}, bf16[512,512]{0,1:T(8,128)(2,1)S(1)}) fusion(f32[512,512]{0,1:T(8,128)} %convolution_bitcast_fusion.2, f32[512,512]{0,1:T(8,128)S(1)} %convolution_bitcast_fusion.1, bf16[512,4096]{1,0:T(8,128)(2,1)} %get-tuple-element.162, ...), kind=kOutput, calls=%fused_computation.22 | convolution fusion | flops 2151677952 | bytes 12058624 | tf_op jit(solution)/shard_map/dot_general | solution.py:141
  130.3 5.6 %fusion.16 = f32[4096,512]{1,0:T(8,128)} fusion(bf16[4096,512]{1,0:T(8,128)(2,1)S(1)} %copy-done.2, bf16[512,512]{0,1:T(8,128)(2,1)S(1)} %get-tuple-element.301), kind=kOutput, calls=%fused_computation.39 | convolution fusion | flops 2147483648 | bytes 13107200 | tf_op jit(solution)/shard_map/dot_general | solution.py:156
  135.9 57.5 %while.13 = (s32[]{:T(128)}, bf16[8,128,128]{2,1,0:T(8,128)(2,1)}, s32[8,3]{0,1:T(4,128)S(1)}, bf16[512,4096]{1,0:T(8,128)(2,1)}, s32[]{:T(128)}, /*index=5*/bf1...) while((s32[]{:T(128)}, bf16[8,128,128]{2,1,0:T(8,128)(2,1)}, ...), condition=%wide.region_4.5_spmd, body=%wide.region_3.4_spmd.sunk | while | flops 50364428 | bytes 952131 | solution.py:188
  137.8 1.1 fusion.43
  141.3 1.7 fusion.44
  145.0 1.1 fusion.43
  148.5 1.8 fusion.44
  152.2 1.1 fusion.43
  155.7 1.7 fusion.44
  159.4 1.1 fusion.43
  162.9 1.7 fusion.44
  166.5 1.1 fusion.43
  170.1 1.7 fusion.44
  173.7 1.1 fusion.43
  177.3 1.7 fusion.44
  184.4 1.7 fusion.44
  191.6 1.7 fusion.44
  193.6 8.9 %add_convert_fusion = bf16[4096,512]{1,0:T(8,128)(2,1)} fusion(f32[4096,512]{1,0:T(8,128)} %fusion.16, bf16[4096,512]{1,0:T(8,128)(2,1)} %get-tuple-element.164, bf16[512,512]{0,1:T(8,128)(2,1)S(1)} %get-tuple-element.353), kind=kOutput, calls=%fused_computation.17 | convolution fusion | flops 2151677952 | bytes 17301504 | tf_op jit(solution)/shard_map/dot_general | solution.py:159
  202.7 6.5 %convolution_convert_fusion = bf16[4096,512]{1,0:T(8,128)(2,1)} fusion(bf16[512,4096]{1,0:T(8,128)(2,1)} %get-tuple-element.162, bf16[512,512]{0,1:T(8,128)(2,1)S(1)} %get-tuple-element.354), kind=kOutput, calls=%fused_computation.18 | convolution fusion | flops 2149580800 | bytes 8912896 | tf_op jit(solution)/shard_map/dot_general | solution.py:149
  209.2 56.3 %all-reduce.3.cloned.1.call-done = bf16[1,8,128,128]{3,2,1,0:T(8,128)(2,1)} async-done(((bf16[1,8,128,128]{3,2,1,0:T(8,128)(2,1)}), bf16[1,8,128,128]{3,2,1,0:T(8,128)(2,1)}) %all-reduce.3.cloned.1.call-update) | async-done | bytes 262160 | tf_op jit(solution)/shard_map/psum | solution.py:192
  265.5 1.5 fusion.15
  267.0 91.0 %reduce-scatter.5.cloned.1.call-done = bf16[128,512]{1,0:T(8,128)(2,1)} async-done(((bf16[4096,512]{1,0:T(8,128)(2,1)}), bf16[128,512]{1,0:T(8,128)(2,1)}) %reduce-scatter.5.cloned.1.call-update) | async-done | bytes 131088 | tf_op jit(solution)/shard_map/reduce_scatter | solution.py:160
  358.0 1.7 copy.34
  359.6 91.1 %reduce-scatter.3.cloned.1.call-done = bf16[128,512]{1,0:T(8,128)(2,1)} async-done(((bf16[4096,512]{1,0:T(8,128)(2,1)}), bf16[128,512]{1,0:T(8,128)(2,1)}) %reduce-scatter.3.cloned.1.call-update) | async-done | bytes 131088 | tf_op jit(solution)/shard_map/reduce_scatter | solution.py:148
  450.8 1.7 copy.33
  (55 shorter events, 22.5 us)
Async XLA Ops:
  7.2 60.2 %all-gather.3.cloned.1.call-start = ((), (), s32[]{:S(2)}) async-start(), calls=%async_computation.2 | async-start | bytes 4325376 | tf_op jit(solution)/shard_map/all_gather | solution.py:133
  7.9 115.8 %all-gather.5.cloned.1.call-start = ((), (), s32[]{:S(2)}) async-start(), calls=%async_computation.4 | async-start | bytes 4325376 | tf_op jit(solution)/shard_map/all_gather | solution.py:140
  8.6 256.9 %all-reduce.3.cloned.1.call-start = ((), (), s32[]{:S(2)}) async-start(), calls=%async_computation.6 | async-start | bytes 524288 | tf_op jit(solution)/shard_map/psum | solution.py:192
  37.9 0.9 copy-start.3
  38.8 0.9 copy-start.4
  39.7 0.9 copy-start.5
  40.6 0.7 copy-start.6
  58.7 2.0 copy-start
  67.3 6.0 %copy-start.1 = (bf16[4096,512]{1,0:T(8,128)(2,1)S(1)}, bf16[4096,512]{1,0:T(8,128)(2,1)}, u32[]{:S(2)}) copy-start(bf16[4096,512]{1,0:T(8,128)(2,1)} %copy-done) | copy-start | bytes 12582916
  67.4 6.0 %copy-start.7 = (bf16[512,4096]{1,0:T(8,128)(2,1)S(1)}, bf16[512,4096]{1,0:T(8,128)(2,1)}, u32[]{:S(2)}) copy-start(bf16[512,4096]{1,0:T(8,128)(2,1)} %all-gather.3.cloned.1.call-done) | copy-start | bytes 12582916
  123.7 6.6 %copy-start.2 = (bf16[4096,512]{1,0:T(8,128)(2,1)S(1)}, bf16[4096,512]{1,0:T(8,128)(2,1)}, u32[]{:S(2)}) copy-start(bf16[4096,512]{1,0:T(8,128)(2,1)} %copy-done) | copy-start | bytes 12582916
  193.4 164.6 %reduce-scatter.5.cloned.1.call-start = ((), (), s32[]{:S(2)}) async-start(), calls=%async_computation.5 | async-start | bytes 4325376 | tf_op jit(solution)/shard_map/reduce_scatter | solution.py:160
  202.6 248.2 %reduce-scatter.3.cloned.1.call-start = ((), (), s32[]{:S(2)}) async-start(), calls=%async_computation.3 | async-start | bytes 4325376 | tf_op jit(solution)/shard_map/reduce_scatter | solution.py:148
  209.2 56.3 %copy-start.8 = (f32[1,1,128,128]{3,2,1,0:T(8,128)S(1)}, f32[1,1,128,128]{3,2,1,0:T(8,128)}, u32[]{:S(2)}) copy-start(f32[1,1,128,128]{3,2,1,0:T(8,128)} %param.25) | copy-start | bytes 196612
  209.2 56.3 %copy-start.9 = (bf16[1,1,128,128]{3,2,1,0:T(8,128)(2,1)S(1)}, bf16[1,1,128,128]{3,2,1,0:T(8,128)(2,1)}, u32[]{:S(2)}) copy-start(bf16[1,1,128,128]{3,2,1,0:T(8,128)(2,1)} %param.27) | copy-start | bytes 98308
  209.2 56.3 %copy-start.10 = (bf16[1,1,128,128]{3,2,1,0:T(8,128)(2,1)S(1)}, bf16[1,1,128,128]{3,2,1,0:T(8,128)(2,1)}, u32[]{:S(2)}) copy-start(bf16[1,1,128,128]{3,2,1,0:T(8,128)(2,1)} %param.26) | copy-start | bytes 98308
Sparse Core Ops, SparseCore 0:
  10.5 56.8 all-gather.2
  69.8 53.8 all-gather.4
  193.5 71.9 all-reduce.2
  269.8 88.1 reduce-scatter.4
  361.8 88.9 reduce-scatter.2

commit v2 on v1

v2 whole, which is shorter than its diff:
```python
import functools

import jax
import jax.numpy as jnp
from jax import lax
from jax.experimental import pallas as pl
from jax.experimental.pallas import tpu as pltpu
from jax.sharding import PartitionSpec as P

BLK = 128
QBLK = 64
ADAM_STEP = 20
SIDE = 4
CORES = 2
SEMAPHORES = 256

beta_one = 0.9
beta_two = 0.999
adam_eps = 1e-08
learn_rate = 0.05

MESH = pl.DeviceIdType.MESH
contract_last = (((1,), (1,)), ((), ()))
contract_first = (((0,), (0,)), ((), ()))


def take_scales(codes, table_ref):
    low = jnp.broadcast_to(table_ref[0:1, :], codes.shape)
    high = jnp.broadcast_to(table_ref[1:2, :], codes.shape)
    within = jnp.bitwise_and(codes, 127)
    from_low = jnp.take_along_axis(low, within, axis=1, mode="promise_in_bounds")
    from_high = jnp.take_along_axis(high, within, axis=1, mode="promise_in_bounds")
    return jnp.where(codes < 128, from_low, from_high)


def scale_tile(levels, upper, lower, block):
    scales = jnp.concatenate(
        [jnp.broadcast_to(upper, (QBLK, BLK)), jnp.broadcast_to(lower, (QBLK, BLK))], axis=0
    )
    base = (levels.astype(jnp.float32) * scales).astype(jnp.bfloat16)
    return (base.astype(jnp.float32) + block.astype(jnp.float32)).astype(jnp.bfloat16)


def layer_kernel(
    groups,
    x_ref, dy_ref, gate_levels, up_levels, down_levels, gate_codes, up_codes, down_codes, table_ref,
    picks, delta_ref, first_ref, second_ref,
    out_ref, input_ref, new_delta, new_first, new_second,
    held, gate_w, up_w, down_w, gate_pre, up_pre, grad_hidden, deltas,
    out_parts, input_parts, out_pair, input_pair, far_one, far_all, near_one, near_all,
    grads, grads_in, send_sem, recv_sem, load_sem,
):
    tokens = x_ref.shape[0]
    hidden_count = gate_w.shape[1] // BLK
    width_count = gate_w.shape[0] // BLK
    tensor = width_count
    half, part = tokens // 2, tokens // 4
    z, t = lax.axis_index("dp"), lax.axis_index("tensor")
    core = lax.rem(t, CORES)
    x = lax.rem(lax.div(t, CORES), SIDE)
    y = lax.div(t, CORES * SIDE)

    def spot(dy, dx, which=None):
        row, col = lax.rem(y + dy, SIDE), lax.rem(x + dx, SIDE)
        return (row * SIDE + col) * CORES + (core if which is None else which)

    other = 1 - core
    sibling = spot(0, 0, other)

    indices, sends = {}, []

    def recv_at(key):
        return indices.setdefault(key, len(indices))

    def push(src, dst, to, key):
        copy = pltpu.make_async_remote_copy(
            src_ref=src, dst_ref=dst, send_sem=send_sem.at[len(sends)],
            recv_sem=recv_sem.at[recv_at(key)], device_id=to, device_id_type=MESH,
        )
        copy.start()
        sends.append(copy)

    def arrived(dst, key):
        pltpu.make_async_remote_copy(
            src_ref=dst, dst_ref=dst, send_sem=send_sem.at[0], recv_sem=recv_sem.at[recv_at(key)],
            device_id=(z, sibling), device_id_type=MESH,
        ).wait_recv()

    loads = [
        pltpu.make_async_copy(src, dst, load_sem.at[at])
        for at, (src, dst) in enumerate(
            ((gate_levels, gate_w), (up_levels, up_w), (down_levels, down_w))
        )
    ]
    for load in loads:
        load.start()
    barrier = pltpu.get_barrier_semaphore()
    partners = [(z, spot(0, 1)), (z, spot(0, 3)), (z, spot(1, 0)), (z, spot(3, 0)), (z, sibling)]
    partners += [(lax.rem(z + step, groups), t) for step in range(1, groups)]
    for partner in partners:
        pl.semaphore_signal(barrier, inc=1, device_id=partner, device_id_type=MESH)
    held[t] = x_ref[...]
    held[tensor + t] = dy_ref[...]
    deltas[z] = delta_ref[0, 0].astype(jnp.bfloat16)
    deltas[groups] = jnp.zeros((BLK, BLK), jnp.bfloat16)
    pl.semaphore_wait(barrier, len(partners))

    def block(g, h, dp, ds, piece=None, which=None):
        at = spot(ds, dp, which) if h == 0 else spot(dp, ds, which)
        rows = pl.ds(h * half, half) if piece is None else pl.ds(h * half + piece * part, part)
        return held.at[g * tensor + at, rows]

    def node(h, dp, ds):
        return (z, spot(ds, dp) if h == 0 else spot(dp, ds))

    def spread(g, h, dp):
        whole = block(g, h, dp, 0)
        push(whole, whole, node(h, 0, 1), ("g", g, h, dp, 3, 0))
        push(whole, whole, node(h, 0, 3), ("g", g, h, dp, 1, 0))
        push(whole, whole, (z, sibling), ("s", g, h, dp, 0))

    def gather_zero(g):
        for h in range(2):
            whole = block(g, h, 0, 0)
            push(whole, whole, node(h, 1, 0), ("g", g, h, 3, 0, 0))
            push(whole, whole, node(h, 3, 0), ("g", g, h, 1, 0, 0))
        for h in range(2):
            spread(g, h, 0)

    def gather_one(g):
        for h in range(2):
            for dp, piece, onward in ((3, 0, 1), (1, 1, 3)):
                arrived(block(g, h, dp, 0), ("g", g, h, dp, 0, 0))
                quarter = block(g, h, dp, 0, piece)
                push(quarter, quarter, node(h, onward, 0), ("g", g, h, 2, 0, piece))
        for h in range(2):
            for dp in (3, 1):
                spread(g, h, dp)

    def gather_two(g):
        for h in range(2):
            for piece in range(2):
                arrived(block(g, h, 2, 0, piece), ("g", g, h, 2, 0, piece))
            spread(g, h, 2)

    def gather_three(g, dp):
        for h in range(2):
            for ds, piece, onward in ((3, 0, 1), (1, 1, 3)):
                whole, quarter = block(g, h, dp, ds), block(g, h, dp, ds, piece)
                arrived(whole, ("g", g, h, dp, ds, 0))
                push(quarter, quarter, node(h, 0, onward), ("g", g, h, dp, 2, piece))
                push(whole, whole, (z, sibling), ("s", g, h, dp, ds))

    def gather_four(g, dp):
        for h in range(2):
            for piece in range(2):
                arrived(block(g, h, dp, 2, piece), ("g", g, h, dp, 2, piece))
            whole = block(g, h, dp, 2)
            push(whole, whole, (z, sibling), ("s", g, h, dp, 2))

    def gather_five(g):
        for h in range(2):
            for dp in range(SIDE):
                for ds in range(SIDE):
                    arrived(block(g, h, dp, ds, None, other), ("s", g, h, dp, ds))

    def wide_weights(which, weight, codes_ref, first_group, last_group):
        @pl.loop(first_group, last_group)
        def _(group):
            for hidden_at in range(hidden_count):
                lanes = pl.ds(hidden_at * BLK, BLK)
                codes = codes_ref[pl.ds(pl.multiple_of(group * 8, 8), 8), lanes]
                scales = take_scales(codes, table_ref)
                for inner in range(4):
                    at = group * 4 + inner
                    rows = pl.ds(pl.multiple_of(at * BLK, BLK), BLK)
                    slot = picks[(which * width_count + at) * hidden_count + hidden_at]
                    weight[rows, lanes] = scale_tile(
                        weight[rows, lanes], scales[2 * inner : 2 * inner + 1],
                        scales[2 * inner + 1 : 2 * inner + 2], deltas[slot],
                    )

    def down_weights(first_at, last_at):
        @pl.loop(first_at, last_at)
        def _(at):
            lanes = pl.ds(pl.multiple_of(at * BLK, BLK), BLK)
            scales = take_scales(down_codes[:, lanes], table_ref)
            for hidden_at in range(hidden_count):
                rows = pl.ds(hidden_at * BLK, BLK)
                slot = picks[(2 * width_count + at) * hidden_count + hidden_at]
                down_w[rows, lanes] = scale_tile(
                    down_w[rows, lanes], scales[2 * hidden_at : 2 * hidden_at + 1],
                    scales[2 * hidden_at + 1 : 2 * hidden_at + 2], deltas[slot],
                )

    def across(first, count):
        return jnp.concatenate([held[first + at] for at in range(count)], axis=1)

    def project(weight, into):
        into[...] = jnp.zeros_like(into)

        @pl.loop(0, width_count // 8)
        def _(step):
            rows = pl.ds(pl.multiple_of(step * 8 * BLK, BLK), 8 * BLK)
            into[...] += jnp.dot(
                across(step * 8, 8), weight[rows, :], preferred_element_type=jnp.float32
            )

    def activate():
        @pl.loop(0, tokens // BLK)
        def _(chunk):
            rows = pl.ds(pl.multiple_of(chunk * BLK, BLK), BLK)
            for at in range(hidden_count):
                lanes = pl.ds(at * BLK, BLK)
                gate, up = gate_pre[rows, lanes], up_pre[rows, lanes]
                sig = 1.0 / (1.0 + jnp.exp(-gate))
                gated = gate * sig
                held[2 * tensor + at, rows] = (gated * up).astype(jnp.bfloat16)
                gate_pre[rows, lanes] = gated
                up_pre[rows, lanes] = up * sig * (1.0 + gate * (1.0 - sig))

    def back_hidden():
        grad_hidden[...] = jnp.zeros_like(grad_hidden)

        @pl.loop(0, width_count // 8)
        def _(step):
            lanes = pl.ds(pl.multiple_of(step * 8 * BLK, BLK), 8 * BLK)
            grad_hidden[...] += lax.dot_general(
                across(tensor + step * 8, 8), down_w[:, lanes], contract_last,
                preferred_element_type=jnp.float32,
            )

        @pl.loop(0, tokens // BLK)
        def _(chunk):
            rows = pl.ds(pl.multiple_of(chunk * BLK, BLK), BLK)
            for at in range(hidden_count):
                lanes = pl.ds(at * BLK, BLK)
                grad = grad_hidden[rows, lanes]
                held[2 * tensor + hidden_count + at, rows] = (grad * up_pre[rows, lanes]).astype(
                    jnp.bfloat16
                )
                held[2 * tensor + 2 * hidden_count + at, rows] = (
                    grad * gate_pre[rows, lanes]
                ).astype(jnp.bfloat16)

    parts, pairs = (out_parts, input_parts), (out_pair, input_pair)

    def share(r, row, col):
        chip = row * SIDE + col
        if r == 0:
            columns = pl.ds(pl.multiple_of(chip * 2 * BLK, 2 * BLK), 2 * BLK)
            return jnp.dot(
                across(2 * tensor, hidden_count), down_w[:, columns],
                preferred_element_type=jnp.float32,
            )
        rows = pl.ds(pl.multiple_of(chip * 2 * BLK, 2 * BLK), 2 * BLK)
        return lax.dot_general(
            across(2 * tensor + hidden_count, hidden_count), gate_w[rows, :], contract_last,
            preferred_element_type=jnp.float32,
        ) + lax.dot_general(
            across(2 * tensor + 2 * hidden_count, hidden_count), up_w[rows, :], contract_last,
            preferred_element_type=jnp.float32,
        )

    def pair_copy(r, row, col, sends_at, recvs_at):
        return pltpu.make_async_remote_copy(
            src_ref=parts[r].at[row, col, other], dst_ref=pairs[r].at[row, col],
            send_sem=send_sem.at[sends_at], recv_sem=recv_sem.at[recvs_at],
            device_id=(z, sibling), device_id_type=MESH,
        )

    pair_at = {}

    def make_parts(r, dy):
        sends_at, recvs_at = len(sends), len(indices)
        row = lax.rem(y + dy, SIDE)
        pair_at[r, dy] = (sends_at, recvs_at)
        for col in range(SIDE):
            recv_at(("p", r, dy, col))
            sends.append(pair_copy(r, row, col, sends_at + col, recvs_at + col))

        @pl.loop(0, SIDE)
        def _(col):
            both = share(r, row, col).astype(jnp.bfloat16)
            parts[r][row, col, 0] = both[:, :BLK]
            parts[r][row, col, 1] = both[:, BLK:]
            pair_copy(r, row, col, sends_at + col, recvs_at + col).start()

    def add_pairs(r, dy):
        sends_at, recvs_at = pair_at[r, dy]
        row = lax.rem(y + dy, SIDE)

        @pl.loop(0, SIDE)
        def _(col):
            pair_copy(r, row, col, sends_at + col, recvs_at + col).wait_recv()
            parts[r][row, col, core] = (
                parts[r][row, col, core].astype(jnp.float32)
                + pairs[r][row, col].astype(jnp.float32)
            ).astype(jnp.bfloat16)

    def line(r, h, df, rows):
        if h == 0:
            return parts[r].at[lax.rem(y + df, SIDE), :, core, rows]
        return parts[r].at[:, lax.rem(x + df, SIDE), core, rows]

    def cell(r, h, dg, rows):
        if h == 0:
            return parts[r].at[y, lax.rem(x + dg, SIDE), core, rows]
        return parts[r].at[lax.rem(y + dg, SIDE), x, core, rows]

    def far(h, df):
        return (z, spot(df, 0) if h == 0 else spot(0, df))

    def near(h, dg):
        return (z, spot(0, dg) if h == 0 else spot(dg, 0))

    def whole_rows(h):
        return pl.ds(h * half, half)

    def part_rows(h, piece):
        return pl.ds(h * half + piece * part, part)

    ways = ((0, 1), (1, 3))

    def reduce_one(r, h):
        for piece, onward in ways:
            push(line(r, h, 2, part_rows(h, piece)), far_one.at[r, h, piece], far(h, onward), ("a", r, h, piece))

    def reduce_two(r, h):
        for piece, onward in ways:
            arrived(far_one.at[r, h, piece], ("a", r, h, piece))
            target = line(r, h, onward, part_rows(h, piece))

            @pl.loop(0, SIDE)
            def _(at):
                target[at] = (
                    target[at].astype(jnp.float32) + far_one[r, h, piece, at].astype(jnp.float32)
                ).astype(jnp.bfloat16)

            push(line(r, h, onward, whole_rows(h)), far_all.at[r, h, piece], far(h, onward), ("b", r, h, piece))

    def reduce_three(r, h):
        for piece in range(2):
            arrived(far_all.at[r, h, piece], ("b", r, h, piece))
        target = line(r, h, 0, whole_rows(h))

        @pl.loop(0, SIDE)
        def _(at):
            target[at] = (
                target[at].astype(jnp.float32)
                + far_all[r, h, 0, at].astype(jnp.float32)
                + far_all[r, h, 1, at].astype(jnp.float32)
            ).astype(jnp.bfloat16)

        for piece, onward in ways:
            push(cell(r, h, 2, part_rows(h, piece)), near_one.at[r, h, piece], near(h, onward), ("c", r, h, piece))

    def reduce_four(r, h):
        for piece, onward in ways:
            arrived(near_one.at[r, h, piece], ("c", r, h, piece))
            target = cell(r, h, onward, part_rows(h, piece))
            target[...] = (
                target[...].astype(jnp.float32) + near_one[r, h, piece].astype(jnp.float32)
            ).astype(jnp.bfloat16)
            push(cell(r, h, onward, whole_rows(h)), near_all.at[r, h, piece], near(h, onward), ("d", r, h, piece))

    def reduce_five(r, h, result):
        for piece in range(2):
            arrived(near_all.at[r, h, piece], ("d", r, h, piece))
        result[pl.ds(h * half, half), :] = (
            cell(r, h, 0, whole_rows(h))[...].astype(jnp.float32)
            + near_all[r, h, 0].astype(jnp.float32)
            + near_all[r, h, 1].astype(jnp.float32)
        ).astype(jnp.bfloat16)

    def block_grads():
        base = 3 * width_count * hidden_count

        @pl.loop(0, groups)
        def _(slot):
            grads[slot] = lax.dot_general(
                held[picks[base + slot]], held[picks[base + groups + slot]], contract_first,
                preferred_element_type=jnp.float32,
            ).astype(jnp.bfloat16)

        for step in range(1, groups):
            to = lax.rem(z + step, groups)
            push(grads.at[to], grads_in.at[step - 1], (to, t), ("h", step))

    def adam():
        total = grads[z].astype(jnp.float32)
        for step in range(1, groups):
            arrived(grads_in.at[step - 1], ("h", step))
            total = total + grads_in[step - 1].astype(jnp.float32)
        moment = beta_one * first_ref[0, 0].astype(jnp.float32) + (1.0 - beta_one) * total
        second = (
            beta_two * second_ref[0, 0].astype(jnp.float32) + (1.0 - beta_two) * total * total
        )
        bias_one = 1.0 - beta_one**ADAM_STEP
        bias_two = 1.0 - beta_two**ADAM_STEP
        step_size = learn_rate * (moment / bias_one) / (jnp.sqrt(second / bias_two) + adam_eps)
        new_delta[0, 0] = delta_ref[0, 0] - step_size
        new_first[0, 0] = moment.astype(jnp.bfloat16)
        new_second[0, 0] = second.astype(jnp.bfloat16)

    gather_zero(0)
    for step in range(1, groups):
        push(deltas.at[z], deltas.at[z], (lax.rem(z + step, groups), t), ("w", step))
    for load in loads:
        load.wait()
    gather_one(0)
    for step in range(1, groups):
        arrived(deltas.at[lax.rem(z + groups - step, groups)], ("w", step))
    wide_weights(0, gate_w, gate_codes, 0, 4)
    gather_two(0)
    gather_three(0, 0)
    wide_weights(0, gate_w, gate_codes, 4, 8)
    gather_three(0, 3)
    gather_three(0, 1)
    gather_zero(1)
    wide_weights(1, up_w, up_codes, 0, 4)
    gather_three(0, 2)
    gather_four(0, 0)
    wide_weights(1, up_w, up_codes, 4, 8)
    for dp in (3, 1, 2):
        gather_four(0, dp)
    gather_one(1)
    gather_five(0)
    project(gate_w, gate_pre)
    gather_two(1)
    gather_three(1, 0)
    project(up_w, up_pre)
    gather_three(1, 3)
    gather_three(1, 1)
    activate()
    gather_three(1, 2)
    gather_four(1, 0)
    down_weights(0, width_count)
    for dp in (3, 1, 2):
        gather_four(1, dp)
    for dy in (2, 1, 3, 0):
        make_parts(0, dy)
    add_pairs(0, 2)
    reduce_one(0, 0)
    for dy in (1, 3, 0):
        add_pairs(0, dy)
    reduce_one(0, 1)
    gather_five(1)
    back_hidden()
    for h in range(2):
        reduce_two(0, h)
    make_parts(1, 2)
    make_parts(1, 1)
    for h in range(2):
        reduce_three(0, h)
    make_parts(1, 3)
    make_parts(1, 0)
    for h in range(2):
        reduce_four(0, h)
    add_pairs(1, 2)
    reduce_one(1, 0)
    for dy in (1, 3, 0):
        add_pairs(1, dy)
    reduce_one(1, 1)
    block_grads()
    for h in range(2):
        reduce_five(0, h, out_ref)
    for h in range(2):
        reduce_two(1, h)
    adam()
    for h in range(2):
        reduce_three(1, h)
    for h in range(2):
        reduce_four(1, h)
    for h in range(2):
        reduce_five(1, h, input_ref)
    for copy in sends:
        copy.wait_send()
    assert len(sends) <= SEMAPHORES and len(indices) <= SEMAPHORES


def slot_picks(pattern, width_count, hidden_count, hidden_first):
    slots = pattern.shape[0]
    matrix, width_at, hidden_at = pattern[:, 0], pattern[:, 1], pattern[:, 2] - hidden_first
    place = (matrix * width_count + width_at) * hidden_count + hidden_at
    tiles = jnp.arange(3 * width_count * hidden_count, dtype=jnp.int32)
    found = jnp.where(
        place[:, None] == tiles[None, :], jnp.arange(slots, dtype=jnp.int32)[:, None], slots
    )
    base = 2 * width_count
    left = jnp.where(matrix == 2, base + hidden_at, width_at)
    right = jnp.where(
        matrix == 2, width_count + width_at, base + (1 + matrix) * hidden_count + hidden_at
    )
    return jnp.concatenate([jnp.min(found, axis=0), left, right])


def local(
    groups,
    activations, cotangent, gate_levels, up_levels, down_levels, gate_scales, up_scales, down_scales,
    scale_table, block_pattern, delta_master, first_moment, second_moment,
):
    tokens = activations.shape[0]
    width, hidden = gate_levels.shape
    width_count, hidden_count = width // BLK, hidden // BLK
    half, part = tokens // 2, tokens // 4
    picks = slot_picks(
        block_pattern[0], width_count, hidden_count, lax.axis_index("tensor") * hidden_count
    )
    vmem = pl.BlockSpec(memory_space=pltpu.VMEM)
    anywhere = pl.BlockSpec(memory_space=pl.ANY)
    narrow, wide = jnp.bfloat16, jnp.float32
    return pl.pallas_call(
        functools.partial(layer_kernel, groups),
        out_shape=[
            jax.ShapeDtypeStruct(v.shape, v.dtype)
            for v in (activations, activations, delta_master, first_moment, second_moment)
        ],
        in_specs=[vmem, vmem, anywhere, anywhere, anywhere, vmem, vmem, vmem, vmem]
        + [pl.BlockSpec(memory_space=pltpu.SMEM), vmem, vmem, vmem],
        out_specs=[vmem] * 5,
        scratch_shapes=[
            pltpu.VMEM((2 * width_count + 3 * hidden_count, tokens, BLK), narrow),
            pltpu.VMEM((width, hidden), narrow),
            pltpu.VMEM((width, hidden), narrow),
            pltpu.VMEM((hidden, width), narrow),
            pltpu.VMEM((tokens, hidden), wide),
            pltpu.VMEM((tokens, hidden), wide),
            pltpu.VMEM((tokens, hidden), wide),
            pltpu.VMEM((groups + 1, BLK, BLK), narrow),
            pltpu.VMEM((SIDE, SIDE, CORES, tokens, BLK), narrow),
            pltpu.VMEM((SIDE, SIDE, CORES, tokens, BLK), narrow),
            pltpu.VMEM((SIDE, SIDE, tokens, BLK), narrow),
            pltpu.VMEM((SIDE, SIDE, tokens, BLK), narrow),
            pltpu.VMEM((2, 2, 2, SIDE, part, BLK), narrow),
            pltpu.VMEM((2, 2, 2, SIDE, half, BLK), narrow),
            pltpu.VMEM((2, 2, 2, part, BLK), narrow),
            pltpu.VMEM((2, 2, 2, half, BLK), narrow),
            pltpu.VMEM((groups, BLK, BLK), narrow),
            pltpu.VMEM((groups - 1, BLK, BLK), narrow),
            pltpu.SemaphoreType.DMA((SEMAPHORES,)),
            pltpu.SemaphoreType.DMA((SEMAPHORES,)),
            pltpu.SemaphoreType.DMA((3,)),
        ],
        compiler_params=pltpu.CompilerParams(
            collective_id=0, has_side_effects=True, vmem_limit_bytes=58 * 1024 * 1024
        ),
        cost_estimate=pl.CostEstimate(
            flops=13_000_000_000, bytes_accessed=14_000_000, transcendentals=262_144
        ),
    )(
        activations, cotangent, gate_levels, up_levels, down_levels, gate_scales, up_scales,
        down_scales, scale_table.reshape(2, 128), picks, delta_master, first_moment, second_moment,
    )


def solution(mesh):
    in_specs = (
        P("dp", "tensor"),
        P("dp", "tensor"),
        P(None, "tensor"),
        P(None, "tensor"),
        P("tensor", None),
        P(None, "tensor"),
        P(None, "tensor"),
        P("tensor", None),
        P(),
        P("tensor", None, None),
        P("tensor", "dp", None, None),
        P("tensor", "dp", None, None),
        P("tensor", "dp", None, None),
    )
    out_specs = (
        P("dp", "tensor"),
        P("dp", "tensor"),
        P("tensor", "dp", None, None),
        P("tensor", "dp", None, None),
        P("tensor", "dp", None, None),
    )
    return jax.shard_map(
        functools.partial(local, mesh.shape["dp"]),
        mesh=mesh, in_specs=in_specs, out_specs=out_specs, check_vma=False,
    )
```

time: 460 us -> 100 us (0.22)
  waiting for transfers between devices: 294 us -> 0 us
  Pallas kernels: 17.4 us -> 90.5 us
  matrix products: 68.6 us -> 0 us
  blocking collectives: 27.5 us -> 0 us
  loops' own time: 21.1 us -> 0 us
  between operations: 13.9 us -> 0.65 us
  local copies, waits for them, and re-layouts: 14.1 us -> 8.04 us
    reduce_scatter x2 -> x0, waiting for transfers between devices: 182 us -> none  [the longest x1 91.1 us: local(): lax.psum_scatter(lax.dot_general(down_w, hidden, (((0,), (1,)), ((), ()))...]
    pallas_call x1, Pallas kernels: 17.4 us -> 90.5 us  [local(): pl.pallas_call(functools.partial(layer_kernel, groups), out_shape=[jax.Sh...]
    dot_general x30 -> x0, matrix products: 68.6 us -> none  [the longest x8 14 us: slot_grad(): lax.dot_general(x_part, gate_part, contract_first, preferred_element_type...]
    psum x1 -> x0, waiting for transfers between devices: 56.3 us -> none  [local(): lax.psum(block_grads.astype(jnp.bfloat16), 'dp').astype(jnp.float32)]
    all_gather x2 -> x0, waiting for transfers between devices: 53.7 us -> none  [the longest x1 47 us: local(): whole_dy = lax.all_gather(cotangent, 'tensor', axis=1, tiled=True)]
    all_gather x1 -> x0, blocking collectives: 27.5 us -> none  [local(): lax.all_gather(delta_master.astype(jnp.bfloat16), 'dp', axis=1, tiled=True)]
    another operation x1 -> x0, loops' own time: 21.1 us -> none  [local(): lax.fori_loop(0, slot_total, slot_grad, jnp.zeros((slot_total, BLK, BLK),...]
    dynamic_slice x8 -> x0, local copies, waits for them, and re-layouts: 4.72 us -> none  [slot_grad(): matrix = pattern[slot_index, 0]]
  transfers between devices with their start and end apart: 5 -> 0, of which waited for: 5 -> 0; matrix products, arithmetic and copies ran while one was open for 6% -> 0% of each run, Pallas kernels for 4% -> 0%
where the time goes in v2:
time: 100 us
  Pallas kernels  90.5 us (90%)
  local copies, waits for them, and re-layouts  8.04 us (8%)
    pallas_call x1, Pallas kernels, local(): pl.pallas_call(functools.partial(layer_kernel, groups), out_shape=[jax.Sh...  90.5 us
    unnamed x6, local copies, waits for them, and re-layouts  8.04 us

profile of v2, /device:TPU:32, one launch (start us, length us, event | category | flops | bytes accessed | tf_op | source)
XLA Modules:
  0.0 100.0 jit_solution(3765163265012948262)
XLA Ops:
  0.6 0.7 copy.20
  1.3 0.1 select_reduce_fusion
  1.4 0.7 pad_add_fusion.picks
  2.1 90.5 %shard_map.164 = (bf16[512,128]{1,0:T(8,128)(2,1)}, bf16[512,128]{1,0:T(8,128)(2,1)}, f32[1,1,128,128]{3,2,1,0:T(8,128)}, bf16[1,1,128,128]{3,2,1,0:T(8,128)(2,1)}, bf16[1,1,128,128]{3,2,1,0:T(8,128)(2,1)}) custom-call(bf16[512,128]{1,0:T(8,128)(2,1)} %x_ref.1, bf16[512,128]{1,0:T(8,128)(2,1)} %dy_ref.1, bf16[4096,512]{1,0:T(8,128)(2,1)} %gate_levels.1, ...), custom_call_target="tpu_custom_call" | custom-call | flops 12999999488 | bytes 14000000 | tf_op jit(solution)/shard_map/pallas_call | solution.py:513
  92.6 1.6 %copy.26 = bf16[512,128]{1,0:T(8,128)(2,1)} copy(bf16[512,128]{1,0:T(8,128)(2,1)} %get-tuple-element.12) | data formatting | bytes 262144
  94.2 1.6 %copy.27 = bf16[512,128]{1,0:T(8,128)(2,1)} copy(bf16[512,128]{1,0:T(8,128)(2,1)} %get-tuple-element.13) | data formatting | bytes 262144
  95.8 1.5 %copy.28 = f32[1,1,128,128]{3,2,1,0:T(8,128)} copy(f32[1,1,128,128]{3,2,1,0:T(8,128)} %get-tuple-element.14) | data formatting | bytes 131072
  97.2 1.4 %copy.29 = bf16[1,1,128,128]{3,2,1,0:T(8,128)(2,1)} copy(bf16[1,1,128,128]{3,2,1,0:T(8,128)(2,1)} %get-tuple-element.15) | data formatting | bytes 65536
  98.6 1.4 %copy.30 = bf16[1,1,128,128]{3,2,1,0:T(8,128)(2,1)} copy(bf16[1,1,128,128]{3,2,1,0:T(8,128)(2,1)} %get-tuple-element.16) | data formatting | bytes 65536
  (2 shorter events, 0.0 us)

commit v3 on v2

--- a/solution.py
+++ b/solution.py
@@ -12,7 +12,7 @@
 ADAM_STEP = 20
 SIDE = 4
 CORES = 2
-SEMAPHORES = 256
+SEMAPHORES = 288
 
 beta_one = 0.9
 beta_two = 0.999
@@ -25,8 +25,8 @@
 
 
 def take_scales(codes, table_ref):
-    low = jnp.broadcast_to(table_ref[0:1, :], codes.shape)
-    high = jnp.broadcast_to(table_ref[1:2, :], codes.shape)
+    low = jnp.broadcast_to(table_ref[0:1, 0:128], codes.shape)
+    high = jnp.broadcast_to(table_ref[0:1, 128:256], codes.shape)
     within = jnp.bitwise_and(codes, 127)
     from_low = jnp.take_along_axis(low, within, axis=1, mode="promise_in_bounds")
     from_high = jnp.take_along_axis(high, within, axis=1, mode="promise_in_bounds")
@@ -43,12 +43,12 @@
 
 def layer_kernel(
     groups,
-    x_ref, dy_ref, gate_levels, up_levels, down_levels, gate_codes, up_codes, down_codes, table_ref,
+    x_ref, dy_ref, gate_levels, up_levels, down_levels, gate_scales, up_scales, down_scales, table_ref,
     picks, delta_ref, first_ref, second_ref,
     out_ref, input_ref, new_delta, new_first, new_second,
-    held, gate_w, up_w, down_w, gate_pre, up_pre, grad_hidden, deltas,
+    held, gate_w, up_w, down_w, gate_codes, up_codes, down_codes, gate_pre, up_pre, grad_hidden, deltas,
     out_parts, input_parts, out_pair, input_pair, far_one, far_all, near_one, near_all,
-    grads, grads_in, send_sem, recv_sem, load_sem,
+    grads, grads_in, send_sem, recv_sem, pair_send, pair_recv, load_sem,
 ):
     tokens = x_ref.shape[0]
     hidden_count = gate_w.shape[1] // BLK
@@ -89,7 +89,12 @@
     loads = [
         pltpu.make_async_copy(src, dst, load_sem.at[at])
         for at, (src, dst) in enumerate(
-            ((gate_levels, gate_w), (up_levels, up_w), (down_levels, down_w))
+            (
+                (x_ref, held.at[t]), (dy_ref, held.at[tensor + t]),
+                (gate_scales, gate_codes), (gate_levels, gate_w),
+                (up_scales, up_codes), (up_levels, up_w),
+                (down_scales, down_codes), (down_levels, down_w),
+            )
         )
     ]
     for load in loads:
@@ -99,10 +104,9 @@
     partners += [(lax.rem(z + step, groups), t) for step in range(1, groups)]
     for partner in partners:
         pl.semaphore_signal(barrier, inc=1, device_id=partner, device_id_type=MESH)
-    held[t] = x_ref[...]
-    held[tensor + t] = dy_ref[...]
     deltas[z] = delta_ref[0, 0].astype(jnp.bfloat16)
     deltas[groups] = jnp.zeros((BLK, BLK), jnp.bfloat16)
+    loads[0].wait()
     pl.semaphore_wait(barrier, len(partners))
 
     def block(g, h, dp, ds, piece=None, which=None):
@@ -230,6 +234,7 @@
                 preferred_element_type=jnp.float32,
             )
 
+    def back_gates():
         @pl.loop(0, tokens // BLK)
         def _(chunk):
             rows = pl.ds(pl.multiple_of(chunk * BLK, BLK), BLK)
@@ -262,116 +267,107 @@
             preferred_element_type=jnp.float32,
         )
 
-    def pair_copy(r, row, col, sends_at, recvs_at):
+    def pair_copy(r, row, col, at):
         return pltpu.make_async_remote_copy(
             src_ref=parts[r].at[row, col, other], dst_ref=pairs[r].at[row, col],
-            send_sem=send_sem.at[sends_at], recv_sem=recv_sem.at[recvs_at],
+            send_sem=pair_send.at[r * SIDE * SIDE + at], recv_sem=pair_recv.at[r * SIDE * SIDE + at],
             device_id=(z, sibling), device_id_type=MESH,
         )
 
-    pair_at = {}
-
-    def make_parts(r, dy):
-        sends_at, recvs_at = len(sends), len(indices)
-        row = lax.rem(y + dy, SIDE)
-        pair_at[r, dy] = (sends_at, recvs_at)
-        for col in range(SIDE):
-            recv_at(("p", r, dy, col))
-            sends.append(pair_copy(r, row, col, sends_at + col, recvs_at + col))
-
-        @pl.loop(0, SIDE)
-        def _(col):
+    def three(at):
+        return at + lax.div(at, 2)
+
+    orders = (
+        (SIDE, lambda at: (2, at)),
+        (SIDE - 1, lambda at: (three(at), 2)),
+        ((SIDE - 1) ** 2, lambda at: (three(lax.div(at, SIDE - 1)), three(lax.rem(at, SIDE - 1)))),
+    )
+
+    def make_parts(r, order):
+        count, steps = orders[order]
+
+        @pl.loop(0, count)
+        def _(at):
+            dy, dx = steps(at)
+            row, col = lax.rem(y + dy, SIDE), lax.rem(x + dx, SIDE)
             both = share(r, row, col).astype(jnp.bfloat16)
             parts[r][row, col, 0] = both[:, :BLK]
             parts[r][row, col, 1] = both[:, BLK:]
-            pair_copy(r, row, col, sends_at + col, recvs_at + col).start()
-
-    def add_pairs(r, dy):
-        sends_at, recvs_at = pair_at[r, dy]
-        row = lax.rem(y + dy, SIDE)
-
-        @pl.loop(0, SIDE)
-        def _(col):
-            pair_copy(r, row, col, sends_at + col, recvs_at + col).wait_recv()
+            pair_copy(r, row, col, dy * SIDE + dx).start()
+
+    def add_pairs(r, order):
+        count, steps = orders[order]
+
+        @pl.loop(0, count)
+        def _(at):
+            dy, dx = steps(at)
+            row, col = lax.rem(y + dy, SIDE), lax.rem(x + dx, SIDE)
+            pair_copy(r, row, col, dy * SIDE + dx).wait()
             parts[r][row, col, core] = (
                 parts[r][row, col, core].astype(jnp.float32)
                 + pairs[r][row, col].astype(jnp.float32)
             ).astype(jnp.bfloat16)
 
-    def line(r, h, df, rows):
-        if h == 0:
-            return parts[r].at[lax.rem(y + df, SIDE), :, core, rows]
-        return parts[r].at[:, lax.rem(x + df, SIDE), core, rows]
-
-    def cell(r, h, dg, rows):
-        if h == 0:
-            return parts[r].at[y, lax.rem(x + dg, SIDE), core, rows]
-        return parts[r].at[lax.rem(y + dg, SIDE), x, core, rows]
-
-    def far(h, df):
-        return (z, spot(df, 0) if h == 0 else spot(0, df))
-
-    def near(h, dg):
-        return (z, spot(0, dg) if h == 0 else spot(dg, 0))
-
-    def whole_rows(h):
-        return pl.ds(h * half, half)
-
-    def part_rows(h, piece):
-        return pl.ds(h * half + piece * part, part)
+    def cell(r, h, df, dg, piece=None):
+        rows = pl.ds(h * half, half) if piece is None else pl.ds(h * half + piece * part, part)
+        dy, dx = (df, dg) if h == 0 else (dg, df)
+        return parts[r].at[lax.rem(y + dy, SIDE), lax.rem(x + dx, SIDE), core, rows]
+
+    def chip(h, df, dg):
+        return (z, spot(df, dg) if h == 0 else spot(dg, df))
+
+    def add_into(target, *terms):
+        total = target[...].astype(jnp.float32)
+        for term in terms:
+            total = total + term[...].astype(jnp.float32)
+        target[...] = total.astype(jnp.bfloat16)
 
     ways = ((0, 1), (1, 3))
+    across_order = (2, 1, 3, 0)
 
     def reduce_one(r, h):
-        for piece, onward in ways:
-            push(line(r, h, 2, part_rows(h, piece)), far_one.at[r, h, piece], far(h, onward), ("a", r, h, piece))
-
-    def reduce_two(r, h):
-        for piece, onward in ways:
-            arrived(far_one.at[r, h, piece], ("a", r, h, piece))
-            target = line(r, h, onward, part_rows(h, piece))
-
-            @pl.loop(0, SIDE)
-            def _(at):
-                target[at] = (
-                    target[at].astype(jnp.float32) + far_one[r, h, piece, at].astype(jnp.float32)
-                ).astype(jnp.bfloat16)
-
-            push(line(r, h, onward, whole_rows(h)), far_all.at[r, h, piece], far(h, onward), ("b", r, h, piece))
-
-    def reduce_three(r, h):
+        for dg in across_order:
+            for piece, onward in ways:
+                push(cell(r, h, 2, dg, piece), far_one.at[r, h, piece, dg], chip(h, onward, 0), ("a", r, h, piece, dg))
+
+    def reduce_two(r, dg):
+        for h in range(2):
+            for piece, onward in ways:
+                landed = far_one.at[r, h, piece, dg]
+                arrived(landed, ("a", r, h, piece, dg))
+                add_into(cell(r, h, onward, dg, piece), landed)
+                push(cell(r, h, onward, dg), far_all.at[r, h, piece, dg], chip(h, onward, 0), ("b", r, h, piece, dg))
+
+    def far_sum(r, h, dg):
         for piece in range(2):
-            arrived(far_all.at[r, h, piece], ("b", r, h, piece))
-        target = line(r, h, 0, whole_rows(h))
-
-        @pl.loop(0, SIDE)
-        def _(at):
-            target[at] = (
-                target[at].astype(jnp.float32)
-                + far_all[r, h, 0, at].astype(jnp.float32)
-                + far_all[r, h, 1, at].astype(jnp.float32)
+            arrived(far_all.at[r, h, piece, dg], ("b", r, h, piece, dg))
+        add_into(cell(r, h, 0, dg), far_all.at[r, h, 0, dg], far_all.at[r, h, 1, dg])
+
+    def reduce_three(r):
+        for h in range(2):
+            far_sum(r, h, 2)
+            for piece, onward in ways:
+                push(cell(r, h, 0, 2, piece), near_one.at[r, h, piece], chip(h, 0, onward), ("c", r, h, piece))
+
+    def reduce_four(r):
+        for h in range(2):
+            for piece, onward in ways:
+                far_sum(r, h, onward)
+                arrived(near_one.at[r, h, piece], ("c", r, h, piece))
+                add_into(cell(r, h, 0, onward, piece), near_one.at[r, h, piece])
+                push(cell(r, h, 0, onward), near_all.at[r, h, piece], chip(h, 0, onward), ("d", r, h, piece))
+
+    def reduce_five(r, result):
+        for h in range(2):
+            far_sum(r, h, 0)
+        for h in range(2):
+            for piece in range(2):
+                arrived(near_all.at[r, h, piece], ("d", r, h, piece))
+            result[pl.ds(h * half, half), :] = (
+                cell(r, h, 0, 0)[...].astype(jnp.float32)
+                + near_all[r, h, 0].astype(jnp.float32)
+                + near_all[r, h, 1].astype(jnp.float32)
             ).astype(jnp.bfloat16)
-
-        for piece, onward in ways:
-            push(cell(r, h, 2, part_rows(h, piece)), near_one.at[r, h, piece], near(h, onward), ("c", r, h, piece))
-
-    def reduce_four(r, h):
-        for piece, onward in ways:
-            arrived(near_one.at[r, h, piece], ("c", r, h, piece))
-            target = cell(r, h, onward, part_rows(h, piece))
-            target[...] = (
-                target[...].astype(jnp.float32) + near_one[r, h, piece].astype(jnp.float32)
-            ).astype(jnp.bfloat16)
-            push(cell(r, h, onward, whole_rows(h)), near_all.at[r, h, piece], near(h, onward), ("d", r, h, piece))
-
-    def reduce_five(r, h, result):
-        for piece in range(2):
-            arrived(near_all.at[r, h, piece], ("d", r, h, piece))
-        result[pl.ds(h * half, half), :] = (
-            cell(r, h, 0, whole_rows(h))[...].astype(jnp.float32)
-            + near_all[r, h, 0].astype(jnp.float32)
-            + near_all[r, h, 1].astype(jnp.float32)
-        ).astype(jnp.bfloat16)
 
     def block_grads():
         base = 3 * width_count * hidden_count
@@ -406,77 +402,85 @@
     gather_zero(0)
     for step in range(1, groups):
         push(deltas.at[z], deltas.at[z], (lax.rem(z + step, groups), t), ("w", step))
-    for load in loads:
+    loads[1].wait()
+    gather_zero(1)
+    gather_one(0)
+    gather_three(0, 0)
+    for load in loads[2:4]:
         load.wait()
-    gather_one(0)
     for step in range(1, groups):
         arrived(deltas.at[lax.rem(z + groups - step, groups)], ("w", step))
-    wide_weights(0, gate_w, gate_codes, 0, 4)
+    wide_weights(0, gate_w, gate_codes, 0, 2)
     gather_two(0)
-    gather_three(0, 0)
-    wide_weights(0, gate_w, gate_codes, 4, 8)
+    wide_weights(0, gate_w, gate_codes, 2, 5)
     gather_three(0, 3)
     gather_three(0, 1)
-    gather_zero(1)
-    wide_weights(1, up_w, up_codes, 0, 4)
+    gather_one(1)
+    wide_weights(0, gate_w, gate_codes, 5, 8)
     gather_three(0, 2)
     gather_four(0, 0)
+    for load in loads[4:6]:
+        load.wait()
+    wide_weights(1, up_w, up_codes, 0, 4)
+    gather_four(0, 3)
+    gather_four(0, 1)
+    gather_three(1, 0)
     wide_weights(1, up_w, up_codes, 4, 8)
-    for dp in (3, 1, 2):
-        gather_four(0, dp)
-    gather_one(1)
+    gather_four(0, 2)
+    gather_two(1)
     gather_five(0)
     project(gate_w, gate_pre)
-    gather_two(1)
-    gather_three(1, 0)
-    project(up_w, up_pre)
     gather_three(1, 3)
     gather_three(1, 1)
+    gather_four(1, 0)
+    project(up_w, up_pre)
+    gather_three(1, 2)
+    gather_four(1, 3)
+    gather_four(1, 1)
     activate()
-    gather_three(1, 2)
-    gather_four(1, 0)
+    for load in loads[6:8]:
+        load.wait()
     down_weights(0, width_count)
-    for dp in (3, 1, 2):
-        gather_four(1, dp)
-    for dy in (2, 1, 3, 0):
-        make_parts(0, dy)
+    gather_four(1, 2)
+    for order in range(3):
+        make_parts(0, order)
+    for order in range(2):
+        add_pairs(0, order)
+    for h in range(2):
+        reduce_one(0, h)
     add_pairs(0, 2)
-    reduce_one(0, 0)
-    for dy in (1, 3, 0):
-        add_pairs(0, dy)
-    reduce_one(0, 1)
     gather_five(1)
     back_hidden()
+    for dg in across_order:
+        reduce_two(0, dg)
+    back_gates()
+    make_parts(1, 0)
+    make_parts(1, 1)
+    reduce_three(0)
+    for order in range(2):
+        add_pairs(1, order)
     for h in range(2):
-        reduce_two(0, h)
+        reduce_one(1, h)
     make_parts(1, 2)
-    make_parts(1, 1)
-    for h in range(2):
-        reduce_three(0, h)
-    make_parts(1, 3)
-    make_parts(1, 0)
-    for h in range(2):
-        reduce_four(0, h)
+    reduce_four(0)
     add_pairs(1, 2)
-    reduce_one(1, 0)
-    for dy in (1, 3, 0):
-        add_pairs(1, dy)
-    reduce_one(1, 1)
+    for dg in across_order:
+        reduce_two(1, dg)
     block_grads()
-    for h in range(2):
-        reduce_five(0, h, out_ref)
-    for h in range(2):
-        reduce_two(1, h)
+    reduce_five(0, out_ref)
+    reduce_three(1)
+    reduce_four(1)
     adam()
-    for h in range(2):
-        reduce_three(1, h)
-    for h in range(2):
-        reduce_four(1, h)
-    for h in range(2):
-        reduce_five(1, h, input_ref)
+    reduce_five(1, input_ref)
     for copy in sends:
         copy.wait_send()
     assert len(sends) <= SEMAPHORES and len(indices) <= SEMAPHORES
+
+
+def hand_over(*refs):
+    count = len(refs) // 2
+    for at in range(count):
+        refs[count + at][...] = refs[at][...]
 
 
 def slot_picks(pattern, width_count, hidden_count, hidden_first):
@@ -510,13 +514,14 @@
     vmem = pl.BlockSpec(memory_space=pltpu.VMEM)
     anywhere = pl.BlockSpec(memory_space=pl.ANY)
     narrow, wide = jnp.bfloat16, jnp.float32
-    return pl.pallas_call(
+    shapes = [
+        jax.ShapeDtypeStruct(v.shape, v.dtype)
+        for v in (activations, activations, delta_master, first_moment, second_moment)
+    ]
+    results = pl.pallas_call(
         functools.partial(layer_kernel, groups),
-        out_shape=[
-            jax.ShapeDtypeStruct(v.shape, v.dtype)
-            for v in (activations, activations, delta_master, first_moment, second_moment)
-        ],
-        in_specs=[vmem, vmem, anywhere, anywhere, anywhere, vmem, vmem, vmem, vmem]
+        out_shape=shapes,
+        in_specs=[anywhere] * 8 + [vmem]
         + [pl.BlockSpec(memory_space=pltpu.SMEM), vmem, vmem, vmem],
         out_specs=[vmem] * 5,
         scratch_shapes=[
@@ -524,6 +529,9 @@
             pltpu.VMEM((width, hidden), narrow),
             pltpu.VMEM((width, hidden), narrow),
             pltpu.VMEM((hidden, width), narrow),
+            pltpu.VMEM(gate_scales.shape, jnp.int32),
+            pltpu.VMEM(up_scales.shape, jnp.int32),
+            pltpu.VMEM(down_scales.shape, jnp.int32),
             pltpu.VMEM((tokens, hidden), wide),
             pltpu.VMEM((tokens, hidden), wide),
             pltpu.VMEM((tokens, hidden), wide),
@@ -540,7 +548,9 @@
             pltpu.VMEM((groups - 1, BLK, BLK), narrow),
             pltpu.SemaphoreType.DMA((SEMAPHORES,)),
             pltpu.SemaphoreType.DMA((SEMAPHORES,)),
-            pltpu.SemaphoreType.DMA((3,)),
+            pltpu.SemaphoreType.DMA((2 * SIDE * SIDE,)),
+            pltpu.SemaphoreType.DMA((2 * SIDE * SIDE,)),
+            pltpu.SemaphoreType.DMA((8,)),
         ],
         compiler_params=pltpu.CompilerParams(
             collective_id=0, has_side_effects=True, vmem_limit_bytes=58 * 1024 * 1024
@@ -550,8 +560,14 @@
         ),
     )(
         activations, cotangent, gate_levels, up_levels, down_levels, gate_scales, up_scales,
-        down_scales, scale_table.reshape(2, 128), picks, delta_master, first_moment, second_moment,
-    )
+        down_scales, scale_table.reshape(1, 256), picks, delta_master, first_moment, second_moment,
+    )
+    return pl.pallas_call(
+        hand_over,
+        out_shape=shapes,
+        in_specs=[vmem] * 5,
+        out_specs=[vmem] * 5,
+    )(*results)
 
 
 def solution(mesh):

time: 100 us -> 87.4 us (0.87); the launches traced: 100 us -> 86.1 us
  local copies, waits for them, and re-layouts: 8.04 us -> 0.68 us
  Pallas kernels: 90.5 us -> 84 us
    unnamed x6 -> x1, local copies, waits for them, and re-layouts: 8.04 us -> 0.68 us
    pallas_call x1 -> x2, Pallas kernels: 90.5 us -> 84 us  [the longest x1 82.3 us: local(): pl.pallas_call(functools.partial(layer_kernel, groups), out_shape=shapes,...]
where the time goes in v3:
time: 87.4 us; the launch traced here: 86.1 us
  Pallas kernels  84 us (96%)
    pallas_call x1, Pallas kernels, local(): pl.pallas_call(functools.partial(layer_kernel, groups), out_shape=shapes,...  82.3 us

profile of v3, /device:TPU:32, one launch (start us, length us, event | category | flops | bytes accessed | tf_op | source)
XLA Modules:
  0.0 86.1 jit_solution(4925328389046459532)
XLA Ops:
  0.6 0.7 copy.20
  1.3 0.1 select_reduce_fusion
  1.4 0.7 pad_add_fusion.picks
  2.1 82.3 %shard_map.164 = (bf16[512,128]{1,0:T(8,128)(2,1)}, bf16[512,128]{1,0:T(8,128)(2,1)}, f32[1,1,128,128]{3,2,1,0:T(8,128)}, bf16[1,1,128,128]{3,2,1,0:T(8,128)(2,1)}, bf16[1,1,128,128]{3,2,1,0:T(8,128)(2,1)}) custom-call(bf16[512,128]{1,0:T(8,128)(2,1)} %x_ref.1, bf16[512,128]{1,0:T(8,128)(2,1)} %dy_ref.1, bf16[4096,512]{1,0:T(8,128)(2,1)} %gate_levels.1, ...), custom_call_target="tpu_custom_call" | custom-call | flops 12999999488 | bytes 14000000 | tf_op jit(solution)/shard_map/pallas_call | solution.py:521
  84.4 1.7 %shard_map.165 = (bf16[512,128]{1,0:T(8,128)(2,1)}, bf16[512,128]{1,0:T(8,128)(2,1)}, f32[1,1,128,128]{3,2,1,0:T(8,128)}, bf16[1,1,128,128]{3,2,1,0:T(8,128)(2,1)}, bf16[1,1,128,128]{3,2,1,0:T(8,128)(2,1)}) custom-call(bf16[512,128]{1,0:T(8,128)(2,1)} %get-tuple-element.10.refs_0_, bf16[512,128]{1,0:T(8,128)(2,1)} %get-tuple-element.11.refs_1_, ...), custom_call_target="tpu_custom_call" | custom-call | tf_op jit(solution)/shard_map/pallas_call | solution.py:565
  (2 shorter events, 0.0 us)

commit v4 on v3

--- a/solution.py
+++ b/solution.py
@@ -12,7 +12,8 @@
 ADAM_STEP = 20
 SIDE = 4
 CORES = 2
-SEMAPHORES = 288
+SENDS = 14
+ARRIVALS = 54
 
 beta_one = 0.9
 beta_two = 0.999
@@ -33,11 +34,14 @@
     return jnp.where(codes < 128, from_low, from_high)
 
 
-def scale_tile(levels, upper, lower, block):
+def scale_tile(levels, upper, lower):
     scales = jnp.concatenate(
         [jnp.broadcast_to(upper, (QBLK, BLK)), jnp.broadcast_to(lower, (QBLK, BLK))], axis=0
     )
-    base = (levels.astype(jnp.float32) * scales).astype(jnp.bfloat16)
+    return (levels.astype(jnp.float32) * scales).astype(jnp.bfloat16)
+
+
+def add_block(base, block):
     return (base.astype(jnp.float32) + block.astype(jnp.float32)).astype(jnp.bfloat16)
 
 
@@ -46,9 +50,9 @@
     x_ref, dy_ref, gate_levels, up_levels, down_levels, gate_scales, up_scales, down_scales, table_ref,
     picks, delta_ref, first_ref, second_ref,
     out_ref, input_ref, new_delta, new_first, new_second,
-    held, gate_w, up_w, down_w, gate_codes, up_codes, down_codes, gate_pre, up_pre, grad_hidden, deltas,
+    first, second, held, gate_w, up_w, down_w, gate_codes, up_codes, down_codes, gate_pre, up_pre, grad_hidden, deltas,
     out_parts, input_parts, out_pair, input_pair, far_one, far_all, near_one, near_all,
-    grads, grads_in, send_sem, recv_sem, pair_send, pair_recv, load_sem,
+    grads, grads_in, send_sem, recv_sem, load_sem,
 ):
     tokens = x_ref.shape[0]
     hidden_count = gate_w.shape[1] // BLK
@@ -67,33 +71,40 @@
     other = 1 - core
     sibling = spot(0, 0, other)
 
-    indices, sends = {}, []
-
-    def recv_at(key):
-        return indices.setdefault(key, len(indices))
-
-    def push(src, dst, to, key):
-        copy = pltpu.make_async_remote_copy(
-            src_ref=src, dst_ref=dst, send_sem=send_sem.at[len(sends)],
-            recv_sem=recv_sem.at[recv_at(key)], device_id=to, device_id_type=MESH,
+    leaving, landing = {}, {}
+
+    def copy_of(src, dst, to, send_key, recv_key):
+        return pltpu.make_async_remote_copy(
+            src_ref=src, dst_ref=dst, send_sem=send_sem.at[leaving.setdefault(send_key, len(leaving))],
+            recv_sem=recv_sem.at[landing.setdefault(recv_key, len(landing))],
+            device_id=to, device_id_type=MESH,
         )
-        copy.start()
-        sends.append(copy)
-
-    def arrived(dst, key):
+
+    def push(src, dst, to, send_key, recv_key):
+        copy_of(src, dst, to, send_key, recv_key).start()
+
+    def arrived(like, recv_key):
         pltpu.make_async_remote_copy(
-            src_ref=dst, dst_ref=dst, send_sem=send_sem.at[0], recv_sem=recv_sem.at[recv_at(key)],
+            src_ref=like, dst_ref=like, send_sem=send_sem.at[0],
+            recv_sem=recv_sem.at[landing.setdefault(recv_key, len(landing))],
             device_id=(z, sibling), device_id_type=MESH,
         ).wait_recv()
+
+    def left(like, send_key):
+        pltpu.make_async_remote_copy(
+            src_ref=like, dst_ref=like, send_sem=send_sem.at[leaving[send_key]],
+            recv_sem=recv_sem.at[0], device_id=(z, sibling), device_id_type=MESH,
+        ).wait_send()
 
     loads = [
         pltpu.make_async_copy(src, dst, load_sem.at[at])
         for at, (src, dst) in enumerate(
             (
                 (x_ref, held.at[t]), (dy_ref, held.at[tensor + t]),
+                (down_scales, down_codes), (down_levels, down_w),
                 (gate_scales, gate_codes), (gate_levels, gate_w),
                 (up_scales, up_codes), (up_levels, up_w),
-                (down_scales, down_codes), (down_levels, down_w),
+                (first_ref, first), (second_ref, second),
             )
         )
     ]
@@ -119,54 +130,55 @@
 
     def spread(g, h, dp):
         whole = block(g, h, dp, 0)
-        push(whole, whole, node(h, 0, 1), ("g", g, h, dp, 3, 0))
-        push(whole, whole, node(h, 0, 3), ("g", g, h, dp, 1, 0))
-        push(whole, whole, (z, sibling), ("s", g, h, dp, 0))
+        push(whole, whole, node(h, 0, 1), ("g", g), ("three", g, dp))
+        push(whole, whole, node(h, 0, 3), ("g", g), ("three", g, dp))
+        push(whole, whole, (z, sibling), ("g", g), ("five", g))
+
+    def blocks_of(g, count):
+        return held.at[pl.ds(g * tensor, count)]
 
     def gather_zero(g):
         for h in range(2):
             whole = block(g, h, 0, 0)
-            push(whole, whole, node(h, 1, 0), ("g", g, h, 3, 0, 0))
-            push(whole, whole, node(h, 3, 0), ("g", g, h, 1, 0, 0))
+            push(whole, whole, node(h, 1, 0), ("g", g), ("one", g))
+            push(whole, whole, node(h, 3, 0), ("g", g), ("one", g))
         for h in range(2):
             spread(g, h, 0)
 
     def gather_one(g):
+        arrived(blocks_of(g, 2), ("one", g))
         for h in range(2):
             for dp, piece, onward in ((3, 0, 1), (1, 1, 3)):
-                arrived(block(g, h, dp, 0), ("g", g, h, dp, 0, 0))
                 quarter = block(g, h, dp, 0, piece)
-                push(quarter, quarter, node(h, onward, 0), ("g", g, h, 2, 0, piece))
+                push(quarter, quarter, node(h, onward, 0), ("g", g), ("two", g))
         for h in range(2):
             for dp in (3, 1):
                 spread(g, h, dp)
 
     def gather_two(g):
-        for h in range(2):
-            for piece in range(2):
-                arrived(block(g, h, 2, 0, piece), ("g", g, h, 2, 0, piece))
+        arrived(blocks_of(g, 1), ("two", g))
+        for h in range(2):
             spread(g, h, 2)
 
     def gather_three(g, dp):
+        arrived(blocks_of(g, 2), ("three", g, dp))
         for h in range(2):
             for ds, piece, onward in ((3, 0, 1), (1, 1, 3)):
-                whole, quarter = block(g, h, dp, ds), block(g, h, dp, ds, piece)
-                arrived(whole, ("g", g, h, dp, ds, 0))
-                push(quarter, quarter, node(h, 0, onward), ("g", g, h, dp, 2, piece))
-                push(whole, whole, (z, sibling), ("s", g, h, dp, ds))
+                quarter = block(g, h, dp, ds, piece)
+                push(quarter, quarter, node(h, 0, onward), ("g", g), ("four", g, dp))
+        for h in range(2):
+            for ds in (3, 1):
+                whole = block(g, h, dp, ds)
+                push(whole, whole, (z, sibling), ("g", g), ("five", g))
 
     def gather_four(g, dp):
-        for h in range(2):
-            for piece in range(2):
-                arrived(block(g, h, dp, 2, piece), ("g", g, h, dp, 2, piece))
+        arrived(blocks_of(g, 1), ("four", g, dp))
+        for h in range(2):
             whole = block(g, h, dp, 2)
-            push(whole, whole, (z, sibling), ("s", g, h, dp, 2))
+            push(whole, whole, (z, sibling), ("g", g), ("five", g))
 
     def gather_five(g):
-        for h in range(2):
-            for dp in range(SIDE):
-                for ds in range(SIDE):
-                    arrived(block(g, h, dp, ds, None, other), ("s", g, h, dp, ds))
+        arrived(blocks_of(g, tensor // 2), ("five", g))
 
     def wide_weights(which, weight, codes_ref, first_group, last_group):
         @pl.loop(first_group, last_group)
@@ -179,31 +191,44 @@
                     at = group * 4 + inner
                     rows = pl.ds(pl.multiple_of(at * BLK, BLK), BLK)
                     slot = picks[(which * width_count + at) * hidden_count + hidden_at]
-                    weight[rows, lanes] = scale_tile(
+                    base = scale_tile(
                         weight[rows, lanes], scales[2 * inner : 2 * inner + 1],
-                        scales[2 * inner + 1 : 2 * inner + 2], deltas[slot],
+                        scales[2 * inner + 1 : 2 * inner + 2],
                     )
-
-    def down_weights(first_at, last_at):
-        @pl.loop(first_at, last_at)
-        def _(at):
-            lanes = pl.ds(pl.multiple_of(at * BLK, BLK), BLK)
-            scales = take_scales(down_codes[:, lanes], table_ref)
-            for hidden_at in range(hidden_count):
-                rows = pl.ds(hidden_at * BLK, BLK)
-                slot = picks[(2 * width_count + at) * hidden_count + hidden_at]
-                down_w[rows, lanes] = scale_tile(
-                    down_w[rows, lanes], scales[2 * hidden_at : 2 * hidden_at + 1],
-                    scales[2 * hidden_at + 1 : 2 * hidden_at + 2], deltas[slot],
-                )
+                    weight[rows, lanes] = add_block(base, deltas[slot])
+
+    def down_base(first_group, last_group):
+        @pl.loop(first_group, last_group)
+        def _(group):
+            for inner in range(4):
+                lanes = pl.ds(pl.multiple_of((group * 4 + inner) * BLK, BLK), BLK)
+                scales = take_scales(down_codes[:, lanes], table_ref)
+                for hidden_at in range(hidden_count):
+                    rows = pl.ds(hidden_at * BLK, BLK)
+                    down_w[rows, lanes] = scale_tile(
+                        down_w[rows, lanes], scales[2 * hidden_at : 2 * hidden_at + 1],
+                        scales[2 * hidden_at + 1 : 2 * hidden_at + 2],
+                    )
+
+    def down_blocks(first_group, last_group):
+        @pl.loop(first_group, last_group)
+        def _(group):
+            for inner in range(4):
+                at = group * 4 + inner
+                lanes = pl.ds(pl.multiple_of(at * BLK, BLK), BLK)
+                for hidden_at in range(hidden_count):
+                    rows = pl.ds(hidden_at * BLK, BLK)
+                    slot = picks[(2 * width_count + at) * hidden_count + hidden_at]
+                    down_w[rows, lanes] = add_block(down_w[rows, lanes], deltas[slot])
 
     def across(first, count):
         return jnp.concatenate([held[first + at] for at in range(count)], axis=1)
 
-    def project(weight, into):
-        into[...] = jnp.zeros_like(into)
-
-        @pl.loop(0, width_count // 8)
+    def project(weight, into, first_step, last_step):
+        if first_step == 0:
+            into[...] = jnp.zeros_like(into)
+
+        @pl.loop(first_step, last_step)
         def _(step):
             rows = pl.ds(pl.multiple_of(step * 8 * BLK, BLK), 8 * BLK)
             into[...] += jnp.dot(
@@ -260,49 +285,51 @@
             )
         rows = pl.ds(pl.multiple_of(chip * 2 * BLK, 2 * BLK), 2 * BLK)
         return lax.dot_general(
-            across(2 * tensor + hidden_count, hidden_count), gate_w[rows, :], contract_last,
-            preferred_element_type=jnp.float32,
-        ) + lax.dot_general(
-            across(2 * tensor + 2 * hidden_count, hidden_count), up_w[rows, :], contract_last,
+            across(2 * tensor + hidden_count, 2 * hidden_count),
+            jnp.concatenate([gate_w[rows, :], up_w[rows, :]], axis=1), contract_last,
             preferred_element_type=jnp.float32,
         )
 
-    def pair_copy(r, row, col, at):
-        return pltpu.make_async_remote_copy(
-            src_ref=parts[r].at[row, col, other], dst_ref=pairs[r].at[row, col],
-            send_sem=pair_send.at[r * SIDE * SIDE + at], recv_sem=pair_recv.at[r * SIDE * SIDE + at],
-            device_id=(z, sibling), device_id_type=MESH,
-        )
-
-    def three(at):
-        return at + lax.div(at, 2)
+    def odd(at):
+        return 1 + 2 * lax.rem(at, 2)
 
     orders = (
-        (SIDE, lambda at: (2, at)),
-        (SIDE - 1, lambda at: (three(at), 2)),
-        ((SIDE - 1) ** 2, lambda at: (three(lax.div(at, SIDE - 1)), three(lax.rem(at, SIDE - 1)))),
+        (4, lambda at: (2, at)),
+        (3, lambda at: (at + lax.div(at, 2), 2)),
+        (4, lambda at: (1 + 2 * lax.div(at, 2), odd(at))),
+        (4, lambda at: (odd(at) * (1 - lax.div(at, 2)), odd(at) * lax.div(at, 2))),
+        (1, lambda at: (at, at)),
     )
 
     def make_parts(r, order):
         count, steps = orders[order]
+        each = 2 if count % 2 == 0 else count
+
+        def some(first):
+            spots = []
+            for at in range(each):
+                dy, dx = steps(first + at)
+                spots.append((lax.rem(y + dy, SIDE), lax.rem(x + dx, SIDE)))
+            for row, col in spots:
+                both = share(r, row, col).astype(jnp.bfloat16)
+                parts[r][row, col, 0] = both[:, :BLK]
+                parts[r][row, col, 1] = both[:, BLK:]
+            for row, col in spots:
+                push(parts[r].at[row, col, other], pairs[r].at[row, col], (z, sibling), ("p", r), ("p", r, order))
+
+        if each == count:
+            some(jnp.int32(0))
+        else:
+            pl.loop(0, count // each)(lambda at: some(at * each))
+
+    def add_pairs(r, order):
+        count, steps = orders[order]
+        arrived(pairs[r].at[0, pl.ds(0, count)], ("p", r, order))
 
         @pl.loop(0, count)
         def _(at):
             dy, dx = steps(at)
             row, col = lax.rem(y + dy, SIDE), lax.rem(x + dx, SIDE)
-            both = share(r, row, col).astype(jnp.bfloat16)
-            parts[r][row, col, 0] = both[:, :BLK]
-            parts[r][row, col, 1] = both[:, BLK:]
-            pair_copy(r, row, col, dy * SIDE + dx).start()
-
-    def add_pairs(r, order):
-        count, steps = orders[order]
-
-        @pl.loop(0, count)
-        def _(at):
-            dy, dx = steps(at)
-            row, col = lax.rem(y + dy, SIDE), lax.rem(x + dx, SIDE)
-            pair_copy(r, row, col, dy * SIDE + dx).wait()
             parts[r][row, col, core] = (
                 parts[r][row, col, core].astype(jnp.float32)
                 + pairs[r][row, col].astype(jnp.float32)
@@ -325,44 +352,43 @@
     ways = ((0, 1), (1, 3))
     across_order = (2, 1, 3, 0)
 
-    def reduce_one(r, h):
+    def reduce_one(r):
         for dg in across_order:
+            for h in range(2):
+                for piece, onward in ways:
+                    push(cell(r, h, 2, dg, piece), far_one.at[r, dg, h, piece], chip(h, onward, 0), ("a", r), ("a", r, dg))
+
+    def reduce_two(r, dg):
+        arrived(far_one.at[r, dg], ("a", r, dg))
+        for h in range(2):
             for piece, onward in ways:
-                push(cell(r, h, 2, dg, piece), far_one.at[r, h, piece, dg], chip(h, onward, 0), ("a", r, h, piece, dg))
-
-    def reduce_two(r, dg):
+                add_into(cell(r, h, onward, dg, piece), far_one.at[r, dg, h, piece])
+                push(cell(r, h, onward, dg), far_all.at[r, dg, h, piece], chip(h, onward, 0), ("b", r), ("b", r, dg))
+
+    def far_sum(r, dg):
+        arrived(far_all.at[r, dg], ("b", r, dg))
+        for h in range(2):
+            add_into(cell(r, h, 0, dg), far_all.at[r, dg, h, 0], far_all.at[r, dg, h, 1])
+
+    def reduce_three(r):
+        far_sum(r, 2)
         for h in range(2):
             for piece, onward in ways:
-                landed = far_one.at[r, h, piece, dg]
-                arrived(landed, ("a", r, h, piece, dg))
-                add_into(cell(r, h, onward, dg, piece), landed)
-                push(cell(r, h, onward, dg), far_all.at[r, h, piece, dg], chip(h, onward, 0), ("b", r, h, piece, dg))
-
-    def far_sum(r, h, dg):
-        for piece in range(2):
-            arrived(far_all.at[r, h, piece, dg], ("b", r, h, piece, dg))
-        add_into(cell(r, h, 0, dg), far_all.at[r, h, 0, dg], far_all.at[r, h, 1, dg])
-
-    def reduce_three(r):
-        for h in range(2):
-            far_sum(r, h, 2)
+                push(cell(r, h, 0, 2, piece), near_one.at[r, h, piece], chip(h, 0, onward), ("c", r), ("c", r))
+
+    def reduce_four(r):
+        far_sum(r, 1)
+        far_sum(r, 3)
+        arrived(near_one.at[r], ("c", r))
+        for h in range(2):
             for piece, onward in ways:
-                push(cell(r, h, 0, 2, piece), near_one.at[r, h, piece], chip(h, 0, onward), ("c", r, h, piece))
-
-    def reduce_four(r):
-        for h in range(2):
-            for piece, onward in ways:
-                far_sum(r, h, onward)
-                arrived(near_one.at[r, h, piece], ("c", r, h, piece))
                 add_into(cell(r, h, 0, onward, piece), near_one.at[r, h, piece])
-                push(cell(r, h, 0, onward), near_all.at[r, h, piece], chip(h, 0, onward), ("d", r, h, piece))
+                push(cell(r, h, 0, onward), near_all.at[r, h, piece], chip(h, 0, onward), ("d", r), ("d", r))
 
     def reduce_five(r, result):
-        for h in range(2):
-            far_sum(r, h, 0)
-        for h in range(2):
-            for piece in range(2):
-                arrived(near_all.at[r, h, piece], ("d", r, h, piece))
+        far_sum(r, 0)
+        arrived(near_all.at[r], ("d", r))
+        for h in range(2):
             result[pl.ds(h * half, half), :] = (
                 cell(r, h, 0, 0)[...].astype(jnp.float32)
                 + near_all[r, h, 0].astype(jnp.float32)
@@ -381,100 +407,115 @@
 
         for step in range(1, groups):
             to = lax.rem(z + step, groups)
-            push(grads.at[to], grads_in.at[step - 1], (to, t), ("h", step))
+            push(grads.at[to], grads_in.at[step - 1], (to, t), ("h",), ("h",))
 
     def adam():
         total = grads[z].astype(jnp.float32)
+        arrived(grads_in, ("h",))
         for step in range(1, groups):
-            arrived(grads_in.at[step - 1], ("h", step))
             total = total + grads_in[step - 1].astype(jnp.float32)
-        moment = beta_one * first_ref[0, 0].astype(jnp.float32) + (1.0 - beta_one) * total
-        second = (
-            beta_two * second_ref[0, 0].astype(jnp.float32) + (1.0 - beta_two) * total * total
+        moment = beta_one * first[0, 0].astype(jnp.float32) + (1.0 - beta_one) * total
+        square = (
+            beta_two * second[0, 0].astype(jnp.float32) + (1.0 - beta_two) * total * total
         )
         bias_one = 1.0 - beta_one**ADAM_STEP
         bias_two = 1.0 - beta_two**ADAM_STEP
-        step_size = learn_rate * (moment / bias_one) / (jnp.sqrt(second / bias_two) + adam_eps)
+        step_size = learn_rate * (moment / bias_one) / (jnp.sqrt(square / bias_two) + adam_eps)
         new_delta[0, 0] = delta_ref[0, 0] - step_size
         new_first[0, 0] = moment.astype(jnp.bfloat16)
-        new_second[0, 0] = second.astype(jnp.bfloat16)
+        new_second[0, 0] = square.astype(jnp.bfloat16)
 
     gather_zero(0)
     for step in range(1, groups):
-        push(deltas.at[z], deltas.at[z], (lax.rem(z + step, groups), t), ("w", step))
-    loads[1].wait()
+        push(deltas.at[z], deltas.at[z], (lax.rem(z + step, groups), t), ("w",), ("w",))
+    for load in loads[1:4]:
+        load.wait()
+    down_base(0, 4)
     gather_zero(1)
+    down_base(4, 8)
     gather_one(0)
     gather_three(0, 0)
-    for load in loads[2:4]:
+    for load in loads[4:]:
         load.wait()
-    for step in range(1, groups):
-        arrived(deltas.at[lax.rem(z + groups - step, groups)], ("w", step))
-    wide_weights(0, gate_w, gate_codes, 0, 2)
     gather_two(0)
-    wide_weights(0, gate_w, gate_codes, 2, 5)
+    arrived(deltas.at[pl.ds(0, groups - 1)], ("w",))
+    wide_weights(0, gate_w, gate_codes, 0, 4)
     gather_three(0, 3)
+    wide_weights(0, gate_w, gate_codes, 4, 8)
     gather_three(0, 1)
     gather_one(1)
-    wide_weights(0, gate_w, gate_codes, 5, 8)
+    wide_weights(1, up_w, up_codes, 0, 4)
+    gather_four(0, 0)
     gather_three(0, 2)
-    gather_four(0, 0)
-    for load in loads[4:6]:
-        load.wait()
-    wide_weights(1, up_w, up_codes, 0, 4)
+    wide_weights(1, up_w, up_codes, 4, 8)
+    gather_three(1, 0)
     gather_four(0, 3)
     gather_four(0, 1)
-    gather_three(1, 0)
-    wide_weights(1, up_w, up_codes, 4, 8)
+    down_blocks(0, 8)
     gather_four(0, 2)
     gather_two(1)
     gather_five(0)
-    project(gate_w, gate_pre)
+    project(gate_w, gate_pre, 0, 2)
     gather_three(1, 3)
     gather_three(1, 1)
+    project(gate_w, gate_pre, 2, 4)
     gather_four(1, 0)
-    project(up_w, up_pre)
+    project(up_w, up_pre, 0, 2)
     gather_three(1, 2)
+    project(up_w, up_pre, 2, 4)
     gather_four(1, 3)
     gather_four(1, 1)
     activate()
-    for load in loads[6:8]:
-        load.wait()
-    down_weights(0, width_count)
+    make_parts(0, 0)
     gather_four(1, 2)
-    for order in range(3):
-        make_parts(0, order)
-    for order in range(2):
-        add_pairs(0, order)
-    for h in range(2):
-        reduce_one(0, h)
-    add_pairs(0, 2)
+    make_parts(0, 1)
+    add_pairs(0, 0)
+    add_pairs(0, 1)
+    reduce_one(0)
     gather_five(1)
     back_hidden()
-    for dg in across_order:
+    back_gates()
+    make_parts(0, 2)
+    add_pairs(0, 2)
+    for dg in (2, 1, 3):
         reduce_two(0, dg)
-    back_gates()
+    make_parts(0, 3)
+    make_parts(0, 4)
+    add_pairs(0, 3)
+    add_pairs(0, 4)
+    reduce_two(0, 0)
     make_parts(1, 0)
     make_parts(1, 1)
     reduce_three(0)
-    for order in range(2):
-        add_pairs(1, order)
-    for h in range(2):
-        reduce_one(1, h)
+    add_pairs(1, 0)
+    add_pairs(1, 1)
+    reduce_one(1)
     make_parts(1, 2)
     reduce_four(0)
+    block_grads()
     add_pairs(1, 2)
-    for dg in across_order:
+    for dg in (2, 1, 3):
         reduce_two(1, dg)
-    block_grads()
+    make_parts(1, 3)
+    make_parts(1, 4)
     reduce_five(0, out_ref)
+    add_pairs(1, 3)
+    add_pairs(1, 4)
+    reduce_two(1, 0)
     reduce_three(1)
     reduce_four(1)
     adam()
     reduce_five(1, input_ref)
-    for copy in sends:
-        copy.wait_send()
-    assert len(sends) <= SEMAPHORES and len(indices) <= SEMAPHORES
+    left(deltas.at[pl.ds(0, groups - 1)], ("w",))
+    left(grads_in, ("h",))
+    for r in range(2):
+        left(blocks_of(r, tensor - 1), ("g", r))
+        left(pairs[r], ("p", r))
+        left(far_one.at[r], ("a", r))
+        left(far_all.at[r], ("b", r))
+        left(near_one.at[r], ("c", r))
+        left(near_all.at[r], ("d", r))
+    assert len(leaving) <= SENDS and len(landing) <= ARRIVALS, (len(leaving), len(landing))
 
 
 def hand_over(*refs):
@@ -522,9 +563,11 @@
         functools.partial(layer_kernel, groups),
         out_shape=shapes,
         in_specs=[anywhere] * 8 + [vmem]
-        + [pl.BlockSpec(memory_space=pltpu.SMEM), vmem, vmem, vmem],
+        + [pl.BlockSpec(memory_space=pltpu.SMEM), vmem, anywhere, anywhere],
         out_specs=[vmem] * 5,
         scratch_shapes=[
+            pltpu.VMEM(first_moment.shape, narrow),
+            pltpu.VMEM(second_moment.shape, narrow),
             pltpu.VMEM((2 * width_count + 3 * hidden_count, tokens, BLK), narrow),
             pltpu.VMEM((width, hidden), narrow),
             pltpu.VMEM((width, hidden), narrow),
@@ -540,17 +583,15 @@
             pltpu.VMEM((SIDE, SIDE, CORES, tokens, BLK), narrow),
             pltpu.VMEM((SIDE, SIDE, tokens, BLK), narrow),
             pltpu.VMEM((SIDE, SIDE, tokens, BLK), narrow),
-            pltpu.VMEM((2, 2, 2, SIDE, part, BLK), narrow),
-            pltpu.VMEM((2, 2, 2, SIDE, half, BLK), narrow),
+            pltpu.VMEM((2, SIDE, 2, 2, part, BLK), narrow),
+            pltpu.VMEM((2, SIDE, 2, 2, half, BLK), narrow),
             pltpu.VMEM((2, 2, 2, part, BLK), narrow),
             pltpu.VMEM((2, 2, 2, half, BLK), narrow),
             pltpu.VMEM((groups, BLK, BLK), narrow),
             pltpu.VMEM((groups - 1, BLK, BLK), narrow),
-            pltpu.SemaphoreType.DMA((SEMAPHORES,)),
-            pltpu.SemaphoreType.DMA((SEMAPHORES,)),
-            pltpu.SemaphoreType.DMA((2 * SIDE * SIDE,)),
-            pltpu.SemaphoreType.DMA((2 * SIDE * SIDE,)),
-            pltpu.SemaphoreType.DMA((8,)),
+            pltpu.SemaphoreType.DMA((SENDS,)),
+            pltpu.SemaphoreType.DMA((ARRIVALS,)),
+            pltpu.SemaphoreType.DMA((10,)),
         ],
         compiler_params=pltpu.CompilerParams(
             collective_id=0, has_side_effects=True, vmem_limit_bytes=58 * 1024 * 1024

time: 87.4 us -> 75 us (0.86)
  Pallas kernels: 84 us -> 72.2 us
    pallas_call x1, Pallas kernels: 82.3 us -> 70.5 us  [local(): pl.pallas_call(functools.partial(layer_kernel, groups), out_shape=shapes,...]
where the time goes in v4:
time: 75 us; the launch traced here: 74.3 us
  Pallas kernels  72.2 us (96%)
  other arithmetic  0.76 us (1%)
    pallas_call x1, Pallas kernels, local(): pl.pallas_call(functools.partial(layer_kernel, groups), out_shape=shapes,...  70.5 us
    pallas_call x1, Pallas kernels, local(): pl.pallas_call(hand_over, out_shape=shapes, in_specs=[vmem] * 5, out_spec...  1.74 us

profile of v4, /device:TPU:32, one launch (start us, length us, event | category | flops | bytes accessed | tf_op | source)
XLA Modules:
  0.0 74.3 jit_solution(14337266755859898102)
XLA Ops:
  0.6 0.7 copy.20
  1.3 0.1 select_reduce_fusion
  1.4 0.7 pad_add_fusion.picks
  2.1 70.5 %shard_map.164 = (bf16[512,128]{1,0:T(8,128)(2,1)}, bf16[512,128]{1,0:T(8,128)(2,1)}, f32[1,1,128,128]{3,2,1,0:T(8,128)}, bf16[1,1,128,128]{3,2,1,0:T(8,128)(2,1)}, bf16[1,1,128,128]{3,2,1,0:T(8,128)(2,1)}) custom-call(bf16[512,128]{1,0:T(8,128)(2,1)} %x_ref.1, bf16[512,128]{1,0:T(8,128)(2,1)} %dy_ref.1, bf16[4096,512]{1,0:T(8,128)(2,1)} %gate_levels.1, ...), custom_call_target="tpu_custom_call" | custom-call | flops 12999999488 | bytes 14000000 | tf_op jit(solution)/shard_map/pallas_call | solution.py:562
  72.6 1.7 %shard_map.165 = (bf16[512,128]{1,0:T(8,128)(2,1)}, bf16[512,128]{1,0:T(8,128)(2,1)}, f32[1,1,128,128]{3,2,1,0:T(8,128)}, bf16[1,1,128,128]{3,2,1,0:T(8,128)(2,1)}, bf16[1,1,128,128]{3,2,1,0:T(8,128)(2,1)}) custom-call(bf16[512,128]{1,0:T(8,128)(2,1)} %get-tuple-element.10.refs_0_, bf16[512,128]{1,0:T(8,128)(2,1)} %get-tuple-element.11.refs_1_, ...), custom_call_target="tpu_custom_call" | custom-call | tf_op jit(solution)/shard_map/pallas_call | solution.py:606
  (2 shorter events, 0.0 us)

commit v5 on v4

--- a/solution.py
+++ b/solution.py
@@ -142,6 +142,8 @@
             whole = block(g, h, 0, 0)
             push(whole, whole, node(h, 1, 0), ("g", g), ("one", g))
             push(whole, whole, node(h, 3, 0), ("g", g), ("one", g))
+
+    def spread_own(g):
         for h in range(2):
             spread(g, h, 0)
 
@@ -426,13 +428,12 @@
         new_second[0, 0] = square.astype(jnp.bfloat16)
 
     gather_zero(0)
+    spread_own(0)
     for step in range(1, groups):
         push(deltas.at[z], deltas.at[z], (lax.rem(z + step, groups), t), ("w",), ("w",))
     for load in loads[1:4]:
         load.wait()
-    down_base(0, 4)
-    gather_zero(1)
-    down_base(4, 8)
+    down_base(0, 8)
     gather_one(0)
     gather_three(0, 0)
     for load in loads[4:]:
@@ -441,68 +442,69 @@
     arrived(deltas.at[pl.ds(0, groups - 1)], ("w",))
     wide_weights(0, gate_w, gate_codes, 0, 4)
     gather_three(0, 3)
+    gather_three(0, 1)
+    gather_zero(1)
     wide_weights(0, gate_w, gate_codes, 4, 8)
-    gather_three(0, 1)
-    gather_one(1)
-    wide_weights(1, up_w, up_codes, 0, 4)
     gather_four(0, 0)
     gather_three(0, 2)
-    wide_weights(1, up_w, up_codes, 4, 8)
-    gather_three(1, 0)
+    spread_own(1)
+    wide_weights(1, up_w, up_codes, 0, 4)
     gather_four(0, 3)
     gather_four(0, 1)
-    down_blocks(0, 8)
+    wide_weights(1, up_w, up_codes, 4, 8)
+    gather_one(1)
     gather_four(0, 2)
-    gather_two(1)
+    down_blocks(0, 4)
+    gather_three(1, 0)
     gather_five(0)
     project(gate_w, gate_pre, 0, 2)
+    gather_two(1)
+    project(gate_w, gate_pre, 2, 4)
+    project(up_w, up_pre, 0, 2)
     gather_three(1, 3)
     gather_three(1, 1)
-    project(gate_w, gate_pre, 2, 4)
+    project(up_w, up_pre, 2, 4)
+    gather_three(1, 2)
     gather_four(1, 0)
-    project(up_w, up_pre, 0, 2)
-    gather_three(1, 2)
-    project(up_w, up_pre, 2, 4)
+    activate()
+    down_blocks(4, 8)
+    make_parts(0, 0)
     gather_four(1, 3)
     gather_four(1, 1)
-    activate()
-    make_parts(0, 0)
+    make_parts(0, 1)
     gather_four(1, 2)
-    make_parts(0, 1)
     add_pairs(0, 0)
     add_pairs(0, 1)
     reduce_one(0)
+    for order in (2, 3, 4):
+        make_parts(0, order)
     gather_five(1)
     back_hidden()
-    back_gates()
-    make_parts(0, 2)
     add_pairs(0, 2)
     for dg in (2, 1, 3):
         reduce_two(0, dg)
-    make_parts(0, 3)
-    make_parts(0, 4)
     add_pairs(0, 3)
     add_pairs(0, 4)
     reduce_two(0, 0)
-    make_parts(1, 0)
-    make_parts(1, 1)
+    back_gates()
+    for order in (0, 1, 2):
+        make_parts(1, order)
     reduce_three(0)
     add_pairs(1, 0)
     add_pairs(1, 1)
     reduce_one(1)
-    make_parts(1, 2)
+    block_grads()
     reduce_four(0)
-    block_grads()
+    make_parts(1, 3)
+    make_parts(1, 4)
     add_pairs(1, 2)
     for dg in (2, 1, 3):
         reduce_two(1, dg)
-    make_parts(1, 3)
-    make_parts(1, 4)
-    reduce_five(0, out_ref)
     add_pairs(1, 3)
     add_pairs(1, 4)
+    reduce_three(1)
     reduce_two(1, 0)
-    reduce_three(1)
+    reduce_five(0, out_ref)
     reduce_four(1)
     adam()
     reduce_five(1, input_ref)

time: 75 us -> 72.3 us (0.964)
  Pallas kernels: 72.2 us -> 70.1 us
    pallas_call x1, Pallas kernels: 70.5 us -> 68.4 us  [local(): pl.pallas_call(functools.partial(layer_kernel, groups), out_shape=shapes,...]
where the time goes in v5:
time: 72.3 us; the launch traced here: 72.2 us
  Pallas kernels  70.1 us (97%)
  other arithmetic  0.76 us (1%)
    pallas_call x1, Pallas kernels, local(): pl.pallas_call(functools.partial(layer_kernel, groups), out_shape=shapes,...  68.4 us
    pallas_call x1, Pallas kernels, local(): pl.pallas_call(hand_over, out_shape=shapes, in_specs=[vmem] * 5, out_spec...  1.74 us

profile of v5, /device:TPU:32, one launch (start us, length us, event | category | flops | bytes accessed | tf_op | source)
XLA Modules:
  0.0 72.2 jit_solution(768956073630208694)
XLA Ops:
  0.6 0.7 copy.20
  1.3 0.1 select_reduce_fusion
  1.4 0.7 pad_add_fusion.picks
  2.1 68.4 %shard_map.164 = (bf16[512,128]{1,0:T(8,128)(2,1)}, bf16[512,128]{1,0:T(8,128)(2,1)}, f32[1,1,128,128]{3,2,1,0:T(8,128)}, bf16[1,1,128,128]{3,2,1,0:T(8,128)(2,1)}, bf16[1,1,128,128]{3,2,1,0:T(8,128)(2,1)}) custom-call(bf16[512,128]{1,0:T(8,128)(2,1)} %x_ref.1, bf16[512,128]{1,0:T(8,128)(2,1)} %dy_ref.1, bf16[4096,512]{1,0:T(8,128)(2,1)} %gate_levels.1, ...), custom_call_target="tpu_custom_call" | custom-call | flops 12999999488 | bytes 14000000 | tf_op jit(solution)/shard_map/pallas_call | solution.py:564
  70.4 1.7 %shard_map.165 = (bf16[512,128]{1,0:T(8,128)(2,1)}, bf16[512,128]{1,0:T(8,128)(2,1)}, f32[1,1,128,128]{3,2,1,0:T(8,128)}, bf16[1,1,128,128]{3,2,1,0:T(8,128)(2,1)}, bf16[1,1,128,128]{3,2,1,0:T(8,128)(2,1)}) custom-call(bf16[512,128]{1,0:T(8,128)(2,1)} %get-tuple-element.10.refs_0_, bf16[512,128]{1,0:T(8,128)(2,1)} %get-tuple-element.11.refs_1_, ...), custom_call_target="tpu_custom_call" | custom-call | tf_op jit(solution)/shard_map/pallas_call | solution.py:608
  (2 shorter events, 0.0 us)

commit v6 on v5

--- a/solution.py
+++ b/solution.py
@@ -250,10 +250,11 @@
                 gate_pre[rows, lanes] = gated
                 up_pre[rows, lanes] = up * sig * (1.0 + gate * (1.0 - sig))
 
-    def back_hidden():
-        grad_hidden[...] = jnp.zeros_like(grad_hidden)
-
-        @pl.loop(0, width_count // 8)
+    def back_hidden(first_step, last_step):
+        if first_step == 0:
+            grad_hidden[...] = jnp.zeros_like(grad_hidden)
+
+        @pl.loop(first_step, last_step)
         def _(step):
             lanes = pl.ds(pl.multiple_of(step * 8 * BLK, BLK), 8 * BLK)
             grad_hidden[...] += lax.dot_general(
@@ -449,17 +450,18 @@
     gather_three(0, 2)
     spread_own(1)
     wide_weights(1, up_w, up_codes, 0, 4)
+    down_blocks(0, 4)
     gather_four(0, 3)
     gather_four(0, 1)
     wide_weights(1, up_w, up_codes, 4, 8)
     gather_one(1)
     gather_four(0, 2)
-    down_blocks(0, 4)
+    down_blocks(4, 8)
     gather_three(1, 0)
     gather_five(0)
     project(gate_w, gate_pre, 0, 2)
+    project(gate_w, gate_pre, 2, 4)
     gather_two(1)
-    project(gate_w, gate_pre, 2, 4)
     project(up_w, up_pre, 0, 2)
     gather_three(1, 3)
     gather_three(1, 1)
@@ -467,22 +469,24 @@
     gather_three(1, 2)
     gather_four(1, 0)
     activate()
-    down_blocks(4, 8)
     make_parts(0, 0)
-    gather_four(1, 3)
-    gather_four(1, 1)
     make_parts(0, 1)
-    gather_four(1, 2)
     add_pairs(0, 0)
     add_pairs(0, 1)
     reduce_one(0)
-    for order in (2, 3, 4):
-        make_parts(0, order)
+    gather_four(1, 3)
+    gather_four(1, 1)
+    make_parts(0, 2)
+    gather_four(1, 2)
+    make_parts(0, 3)
+    make_parts(0, 4)
     gather_five(1)
-    back_hidden()
+    back_hidden(0, 2)
+    reduce_two(0, 2)
     add_pairs(0, 2)
-    for dg in (2, 1, 3):
-        reduce_two(0, dg)
+    reduce_two(0, 1)
+    reduce_two(0, 3)
+    back_hidden(2, 4)
     add_pairs(0, 3)
     add_pairs(0, 4)
     reduce_two(0, 0)
@@ -494,15 +498,16 @@
     add_pairs(1, 1)
     reduce_one(1)
     block_grads()
+    make_parts(1, 3)
+    reduce_two(1, 2)
+    add_pairs(1, 2)
+    reduce_two(1, 1)
+    reduce_two(1, 3)
     reduce_four(0)
-    make_parts(1, 3)
     make_parts(1, 4)
-    add_pairs(1, 2)
-    for dg in (2, 1, 3):
-        reduce_two(1, dg)
+    reduce_three(1)
     add_pairs(1, 3)
     add_pairs(1, 4)
-    reduce_three(1)
     reduce_two(1, 0)
     reduce_five(0, out_ref)
     reduce_four(1)

time: 72.3 us -> 72.1 us (level)
  no operation moved by 1% of the time
where the time goes in v6:
time: 72.1 us; the launch traced here: 71.9 us
  Pallas kernels  69.8 us (97%)
  other arithmetic  0.76 us (1%)
    pallas_call x1, Pallas kernels, local(): pl.pallas_call(functools.partial(layer_kernel, groups), out_shape=shapes,...  68.1 us
    pallas_call x1, Pallas kernels, local(): pl.pallas_call(hand_over, out_shape=shapes, in_specs=[vmem] * 5, out_spec...  1.74 us

profile of v6, /device:TPU:32, one launch (start us, length us, event | category | flops | bytes accessed | tf_op | source)
XLA Modules:
  0.0 71.9 jit_solution(14189057314122759805)
XLA Ops:
  0.6 0.7 copy.20
  1.3 0.1 select_reduce_fusion
  1.4 0.7 pad_add_fusion.picks
  2.1 68.1 %shard_map.164 = (bf16[512,128]{1,0:T(8,128)(2,1)}, bf16[512,128]{1,0:T(8,128)(2,1)}, f32[1,1,128,128]{3,2,1,0:T(8,128)}, bf16[1,1,128,128]{3,2,1,0:T(8,128)(2,1)}, bf16[1,1,128,128]{3,2,1,0:T(8,128)(2,1)}) custom-call(bf16[512,128]{1,0:T(8,128)(2,1)} %x_ref.1, bf16[512,128]{1,0:T(8,128)(2,1)} %dy_ref.1, bf16[4096,512]{1,0:T(8,128)(2,1)} %gate_levels.1, ...), custom_call_target="tpu_custom_call" | custom-call | flops 12999999488 | bytes 14000000 | tf_op jit(solution)/shard_map/pallas_call | solution.py:569
  70.2 1.7 %shard_map.165 = (bf16[512,128]{1,0:T(8,128)(2,1)}, bf16[512,128]{1,0:T(8,128)(2,1)}, f32[1,1,128,128]{3,2,1,0:T(8,128)}, bf16[1,1,128,128]{3,2,1,0:T(8,128)(2,1)}, bf16[1,1,128,128]{3,2,1,0:T(8,128)(2,1)}) custom-call(bf16[512,128]{1,0:T(8,128)(2,1)} %get-tuple-element.10.refs_0_, bf16[512,128]{1,0:T(8,128)(2,1)} %get-tuple-element.11.refs_1_, ...), custom_call_target="tpu_custom_call" | custom-call | tf_op jit(solution)/shard_map/pallas_call | solution.py:613
  (2 shorter events, 0.0 us)
